TPU v7x, 256 devices: a whole 4x4x8 slice. The times are simulated.
256 devices in a mesh: pair: 64 (over z, x, core), occ: 4 (over y).
Axes of the slice: x: 4, y: 4, z: 8, core: 2. Of those that a mesh axis runs over, the one named last changes fastest.
Arguments:
- amplitudes: bfloat16 [256, 256, 128], P('pair', 'occ'), may hold values from -6 to 6
- vectors: bfloat16 [256, 5120, 128], P('pair', 'occ'), may hold values from -0.078125 to 0.078125
- pair_count: int32 [256], P('pair'), may hold values from 64 to 128
- tile_map: int32 [256, 32], replicated, may hold values from 0 to 255, as said below
Outputs:
- residual: bfloat16 [256, 256, 128], P('pair', 'occ')
Inputs may be any that keep to these rules, and one draw needn't show every extreme that they name: `tile_map`: entries of a row are distinct. The rows of one index of pair (blocks d * 4 to (d + 1) * 4 - 1) name every block of that index and exactly one block of every other index of pair.
All inputs are finite; a program needn't handle non-finite values.
Results may differ from a plain program's by a relative error of at most 0.001.
Values may be sent and summed in bfloat16 or wider, within the bound.
A program may use at most 128 MiB of HBM per device.

v0:
```python
import jax
import jax.numpy as jnp
from jax import lax
from jax.sharding import PartitionSpec as P


def body(amplitudes, vectors, pair_count, tile_map):
    blocks = vectors.shape[0]
    slots = vectors.shape[2]
    devices = lax.axis_size("pair")
    me = lax.axis_index("pair")
    iota_slots = lax.broadcasted_iota(jnp.int32, (blocks, 1, slots), 2)
    live = iota_slots < pair_count[:, None, None]
    masked = jnp.where(live, vectors, jnp.zeros_like(vectors))
    own_amp = lax.all_gather(amplitudes, "occ", axis=1, tiled=True)
    rows_map = tile_map.reshape(devices, -1)
    holders = rows_map // blocks
    chosen = jnp.where(holders == me, rows_map % blocks, -1)
    wanted = jnp.clip(jnp.max(chosen, axis=1), 0, blocks - 1)
    sent_vec = jnp.take(masked, wanted, axis=0)
    sent_amps = jnp.take(amplitudes, wanted, axis=0)
    got_vec, part_amp = (
        lax.all_to_all(sent_vec, "pair", split_axis=0, concat_axis=0, tiled=True),
        lax.all_to_all(sent_amps, "pair", split_axis=0, concat_axis=0, tiled=True),
    )
    got_amp = lax.all_gather(part_amp, "occ", axis=1, tiled=True)
    pool_vec = jnp.concatenate([masked, got_vec], axis=0)
    pool_amp = jnp.concatenate([own_amp, got_amp], axis=0)
    local_map = lax.dynamic_slice_in_dim(tile_map, me * blocks, blocks, 0)
    source = local_map // blocks
    position = jnp.where(source == me, local_map % blocks, blocks + source)

    def one_row(item):
        left, index = item
        partner_vec = jnp.take(pool_vec, index, axis=0)
        tiles = jnp.einsum("ks,jkt->jst", left, partner_vec, preferred_element_type=jnp.float32)
        partner_amp = jnp.take(pool_amp, index, axis=0).astype(jnp.float32)
        return jnp.einsum("jit,jst->is", partner_amp, tiles, precision=lax.Precision.HIGHEST)

    partials = lax.map(one_row, (masked, position))
    return lax.psum_scatter(partials, "occ", scatter_dimension=1, tiled=True).astype(jnp.bfloat16)


def solution(mesh):
    return jax.shard_map(
        body,
        mesh=mesh,
        in_specs=(P("pair", "occ", None), P("pair", "occ", None), P("pair"), P()),
        out_specs=P("pair", "occ", None),
        check_vma=False,
    )
```

profile of v0, /device:TPU:1, one launch (start us, length us, event | category | flops | bytes accessed | tf_op | source)
XLA Modules:
  0.0 686.9 jit_solution(17579404338683538626)
XLA Ops:
  7.6 1.6 gather_fusion.2
  9.2 1.1 broadcast_select_fusion.2
  10.4 13.0 %all-to-all-start = ((bf16[64,64,128]{2,1,0:T(8,128)(2,1)}), bf16[64,64,128]{2,1,0:T(8,128)(2,1)S(1)}, u32[]{:S(2)}, u32[]{:S(2)}) async-start(bf16[64,64,128]{2,1,0:T(8,128)(2,1)} %broadcast_select_fusion.2), calls=%async_computation | async-start | bytes 2097152 | tf_op jit(solution)/shard_map/all_to_all | solution.py:24
  23.4 1.4 broadcast_select_fusion.1
  24.9 8.9 %gather_fusion.3 = bf16[64,1280,128]{2,1,0:T(8,128)(2,1)} fusion(bf16[4,1280,128]{2,1,0:T(8,128)(2,1)S(1)} %broadcast_select_fusion.1, s32[1024]{0:T(1024)S(1)} %pad_clamp_fusion.1), kind=kCustom, calls=%fused_computation.3 | custom fusion | bytes 41943296 | tf_op jit(solution)/shard_map/jit(_take)/gather | solution.py:20
  33.7 17.7 %broadcast_select_fusion = bf16[64,1280,128]{2,1,0:T(8,128)(2,1)} fusion(bf16[64,1280,128]{2,1,0:T(8,128)(2,1)} %gather_fusion.3, pred[64]{0:T(512)(128)(4,1)S(1)} %compare_and_fusion.1), kind=kLoop, calls=%fused_computation.27 | loop fusion | flops 10485760 | bytes 41943104 | tf_op jit(solution)/shard_map/jit(_take)/select_n | solution.py:20
  51.5 1.0 copy-done.1
  52.5 10.5 %all-to-all-start.1 = ((bf16[64,1280,128]{2,1,0:T(8,128)(2,1)}), bf16[64,1280,128]{2,1,0:T(8,128)(2,1)}, u32[]{:S(2)}, u32[]{:S(2)}) async-start(bf16[64,1280,128]{2,1,0:T(8,128)(2,1)} %broadcast_select_fusion), calls=%async_computation.1 | async-start | bytes 41943040 | tf_op jit(solution)/shard_map/all_to_all | solution.py:23
  64.0 11.1 %all_gather.6 = bf16[4,256,128]{2,1,0:T(8,128)(2,1)S(1)} all-gather(bf16[4,64,128]{2,1,0:T(8,128)(2,1)S(1)} %copy-done), channel_id=1, replica_groups=mesh['pair'=64,'occ'=4] {'occ'}, dimensions={1}, use_global_device_ids=true | all-gather | bytes 327680 | tf_op jit(solution)/shard_map/all_gather | solution.py:15
  75.1 42.5 %all-gather.2.cloned.1.call-done = bf16[64,256,128]{2,1,0:T(8,128)(2,1)} async-done(((bf16[64,64,128]{2,1,0:T(8,128)(2,1)}), bf16[64,256,128]{2,1,0:T(8,128)(2,1)}) %all-gather.2.cloned.1.call-update) | async-done | bytes 4194320 | tf_op jit(solution)/shard_map/all_gather | solution.py:26
  117.6 4.7 pad_maximum_fusion.1
  122.3 397.2 %all-to-all-done.1 = bf16[64,1280,128]{2,1,0:T(8,128)(2,1)} async-done(((bf16[64,1280,128]{2,1,0:T(8,128)(2,1)}), bf16[64,1280,128]{2,1,0:T(8,128)(2,1)}, u32[]{:S(2)}, u32[]{:S(2)}) %all-to-all-start.1) | async-done | bytes 20971552 | tf_op jit(solution)/shard_map/all_to_all | solution.py:23
  519.6 19.1 %pad_maximum_fusion = bf16[68,1280,128]{2,1,0:T(8,128)(2,1)} fusion(bf16[64,1280,128]{2,1,0:T(8,128)(2,1)} %all-to-all-done.1, bf16[4,1280,128]{2,1,0:T(8,128)(2,1)S(1)} %broadcast_select_fusion.1), kind=kLoop, calls=%fused_computation.26 | loop fusion | flops 11141120 | bytes 44564480 | tf_op jit(solution)/shard_map/concatenate | solution.py:27
  538.7 110.7 %while.10 = (s32[]{:T(128)}, f32[4,256,128]{2,1,0:T(8,128)}, s32[4,32]{1,0:T(4,128)S(1)}, bf16[68,256,128]{2,1,0:T(8,128)(2,1)}, bf16[68,1280,128]{2,1,0:T(8,128...) while((s32[]{:T(128)}, f32[4,256,128]{2,1,0:T(8,128)}, s32[4,32]{1,0:T(4,128)S(1)}, ...), condition=%wide.region_3.4_spmd, body=%wide.region_2.3_spmd.sunk | while | flops 2959082752 | bytes 42407832 | solution.py:40
  538.7 13.3 %gather_fusion = bf16[32,1280,128]{2,1,0:T(8,128)(2,1)} fusion(bf16[68,1280,128]{2,1,0:T(8,128)(2,1)} %get-tuple-element.105, s32[1024]{0:T(1024)S(1)} %pad_clamp_fusion.3), kind=kCustom, calls=%fused_computation.1.clone.1 | custom fusion | bytes 20971648 | tf_op jit(solution)/shard_map/while/body/eval_jaxpr/jit(_take)/gather | solution.py:35
  552.0 7.0 %fusion.45 = f32[32,128,128]{1,2,0:T(8,128)} fusion(bf16[32,1280,128]{2,1,0:T(8,128)(2,1)} %gather_fusion, pred[32]{0:T(512)(128)(4,1)S(1)} %compare_and_fusion.3, bf16[4,1280,128]{2,1,0:T(8,128)(2,1)S(1)} %get-tuple-element.106, s32[]{:T(128)} %get-tuple-element.94), kind=kOutput, calls=%fused_computation.4.clone.1 | convolution fusion | flops 1347420160 | bytes 12911108 | tf_op jit(solution)/shard_map/while/body/eval_jaxpr/ks,jkt->jst/dot_general | solution.py:36
  559.0 3.2 gather_fusion.1
  562.2 4.1 fusion.46
  566.4 13.3 %gather_fusion = bf16[32,1280,128]{2,1,0:T(8,128)(2,1)} fusion(bf16[68,1280,128]{2,1,0:T(8,128)(2,1)} %get-tuple-element.105, s32[1024]{0:T(1024)S(1)} %pad_clamp_fusion.3), kind=kCustom, calls=%fused_computation.1.clone.1 | custom fusion | bytes 20971648 | tf_op jit(solution)/shard_map/while/body/eval_jaxpr/jit(_take)/gather | solution.py:35
  579.7 7.0 %fusion.45 = f32[32,128,128]{1,2,0:T(8,128)} fusion(bf16[32,1280,128]{2,1,0:T(8,128)(2,1)} %gather_fusion, pred[32]{0:T(512)(128)(4,1)S(1)} %compare_and_fusion.3, bf16[4,1280,128]{2,1,0:T(8,128)(2,1)S(1)} %get-tuple-element.106, s32[]{:T(128)} %get-tuple-element.94), kind=kOutput, calls=%fused_computation.4.clone.1 | convolution fusion | flops 1347420160 | bytes 12911108 | tf_op jit(solution)/shard_map/while/body/eval_jaxpr/ks,jkt->jst/dot_general | solution.py:36
  586.7 3.2 gather_fusion.1
  589.9 4.1 fusion.46
  594.0 13.3 %gather_fusion = bf16[32,1280,128]{2,1,0:T(8,128)(2,1)} fusion(bf16[68,1280,128]{2,1,0:T(8,128)(2,1)} %get-tuple-element.105, s32[1024]{0:T(1024)S(1)} %pad_clamp_fusion.3), kind=kCustom, calls=%fused_computation.1.clone.1 | custom fusion | bytes 20971648 | tf_op jit(solution)/shard_map/while/body/eval_jaxpr/jit(_take)/gather | solution.py:35
  607.3 7.0 %fusion.45 = f32[32,128,128]{1,2,0:T(8,128)} fusion(bf16[32,1280,128]{2,1,0:T(8,128)(2,1)} %gather_fusion, pred[32]{0:T(512)(128)(4,1)S(1)} %compare_and_fusion.3, bf16[4,1280,128]{2,1,0:T(8,128)(2,1)S(1)} %get-tuple-element.106, s32[]{:T(128)} %get-tuple-element.94), kind=kOutput, calls=%fused_computation.4.clone.1 | convolution fusion | flops 1347420160 | bytes 12911108 | tf_op jit(solution)/shard_map/while/body/eval_jaxpr/ks,jkt->jst/dot_general | solution.py:36
  614.3 3.2 gather_fusion.1
  617.5 4.1 fusion.46
  621.7 13.3 %gather_fusion = bf16[32,1280,128]{2,1,0:T(8,128)(2,1)} fusion(bf16[68,1280,128]{2,1,0:T(8,128)(2,1)} %get-tuple-element.105, s32[1024]{0:T(1024)S(1)} %pad_clamp_fusion.3), kind=kCustom, calls=%fused_computation.1.clone.1 | custom fusion | bytes 20971648 | tf_op jit(solution)/shard_map/while/body/eval_jaxpr/jit(_take)/gather | solution.py:35
  635.0 7.0 %fusion.45 = f32[32,128,128]{1,2,0:T(8,128)} fusion(bf16[32,1280,128]{2,1,0:T(8,128)(2,1)} %gather_fusion, pred[32]{0:T(512)(128)(4,1)S(1)} %compare_and_fusion.3, bf16[4,1280,128]{2,1,0:T(8,128)(2,1)S(1)} %get-tuple-element.106, s32[]{:T(128)} %get-tuple-element.94), kind=kOutput, calls=%fused_computation.4.clone.1 | convolution fusion | flops 1347420160 | bytes 12911108 | tf_op jit(solution)/shard_map/while/body/eval_jaxpr/ks,jkt->jst/dot_general | solution.py:36
  642.0 3.2 gather_fusion.1
  645.2 4.1 fusion.46
  649.4 29.2 %reduce-scatter.2.cloned.1.call-done = f32[4,64,128]{2,1,0:T(8,128)} async-done(((f32[4,256,128]{2,1,0:T(8,128)}), f32[4,64,128]{2,1,0:T(8,128)}) %reduce-scatter.2.cloned.1.call-update) | async-done | bytes 131088 | tf_op jit(solution)/shard_map/reduce_scatter | solution.py:41
  678.5 1.5 convert_element_type.4
  (35 shorter events, 2.2 us)
Async XLA Ops:
  6.5 16.8 %copy-start.3 = (s32[4]{0:T(128)S(1)}, s32[4]{0:T(128)}, u32[]{:S(2)}) copy-start(s32[4]{0:T(128)} %param.8) | copy-start | bytes 52
  10.4 41.1 %all-to-all-start = ((bf16[64,64,128]{2,1,0:T(8,128)(2,1)}), bf16[64,64,128]{2,1,0:T(8,128)(2,1)S(1)}, u32[]{:S(2)}, u32[]{:S(2)}) async-start(bf16[64,64,128]{2,1,0:T(8,128)(2,1)} %broadcast_select_fusion.2), calls=%async_computation | async-start | bytes 2097152 | tf_op jit(solution)/shard_map/all_to_all | solution.py:24
  51.5 1.0 copy-start.1
  51.5 12.3 %copy-start.2 = (s32[256,32]{0,1:T(8,128)S(1)}, s32[256,32]{0,1:T(8,128)}, u32[]{:S(2)}) copy-start(s32[256,32]{0,1:T(8,128)} %param.9) | copy-start | bytes 98308
  51.5 12.5 %copy-start = (bf16[4,64,128]{2,1,0:T(8,128)(2,1)S(1)}, bf16[4,64,128]{2,1,0:T(8,128)(2,1)}, u32[]{:S(2)}) copy-start(bf16[4,64,128]{2,1,0:T(8,128)(2,1)} %param.6) | copy-start | bytes 196612
  52.5 467.1 %all-to-all-start.1 = ((bf16[64,1280,128]{2,1,0:T(8,128)(2,1)}), bf16[64,1280,128]{2,1,0:T(8,128)(2,1)}, u32[]{:S(2)}, u32[]{:S(2)}) async-start(bf16[64,1280,128]{2,1,0:T(8,128)(2,1)} %broadcast_select_fusion), calls=%async_computation.1 | async-start | bytes 41943040 | tf_op jit(solution)/shard_map/all_to_all | solution.py:23
  63.0 54.6 %all-gather.2.cloned.1.call-start = ((), (), s32[]{:S(2)}) async-start(), calls=%async_computation.3 | async-start | bytes 5242880 | tf_op jit(solution)/shard_map/all_gather | solution.py:26
  63.7 614.8 %reduce-scatter.2.cloned.1.call-start = ((), (), s32[]{:S(2)}) async-start(), calls=%async_computation.4 | async-start | bytes 655360 | tf_op jit(solution)/shard_map/reduce_scatter | solution.py:41
Sparse Core Ops, SparseCore 0:
  65.6 51.9 all-gather.1
  649.5 29.0 reduce-scatter.1
where the time goes:
time: 689 us; the launch traced here: 687 us
  waiting for transfers between devices  470 us (68%)
  local copies, waits for them, and re-layouts  77.7 us (11%)
  other arithmetic  46.8 us (7%)
  matrix products  44.5 us (6%)
  starting transfers between devices  23.6 us (3%)
  between operations  13.5 us (2%)
  blocking collectives  11.1 us (2%)
    all_to_all x1, waiting for transfers between devices, body(): lax.all_to_all(sent_vec, 'pair', split_axis=0, concat_axis=0, tiled=True)  397 us
    gather x4, local copies, waits for them, and re-layouts, one_row(): partner_vec = jnp.take(pool_vec, index, axis=0)  53.1 us
    all_gather x1, waiting for transfers between devices, body(): got_amp = lax.all_gather(part_amp, 'occ', axis=1, tiled=True)  42.5 us
    reduce_scatter x1, waiting for transfers between devices, body(): lax.psum_scatter(partials, 'occ', scatter_dimension=1, tiled=True)  29.2 us
    dot_general x4, matrix products, one_row(): jnp.einsum('ks,jkt->jst', left, partner_vec, preferred_element_type=jnp.f...  28 us
    concatenate x1, other arithmetic, body(): pool_vec = jnp.concatenate([masked, got_vec], axis=0)  19.1 us
    select_n x2, other arithmetic, body(): sent_vec = jnp.take(masked, wanted, axis=0)  17.7 us
    dot_general x4, matrix products, one_row(): jnp.einsum('jit,jst->is', partner_amp, tiles, precision=lax.Precision.HIG...  16.5 us
  transfers between devices with their start and end apart: 4, of which 3 were waited for; matrix products, arithmetic and copies ran while one was open for 5% of the time, Pallas kernels for 0%

commit v1 on v0

v1 whole, which is shorter than its diff:
```python
import jax
import jax.numpy as jnp
from jax import lax
from jax.sharding import Mesh, PartitionSpec as P

NZ, NX, NC, NY = 8, 4, 2, 4
ROWS = 16


def split(x):
    hi = lax.reduce_precision(x, 8, 7)
    return hi.astype(jnp.bfloat16), (x - hi).astype(jnp.bfloat16)


def body(amplitudes, vectors, pair_count, tile_map):
    blocks, occ, slots = amplitudes.shape
    total = tile_map.shape[0]
    live = lax.broadcasted_iota(jnp.int32, (blocks, 1, slots), 2) < pair_count[:, None, None]

    vec = lax.all_to_all(vectors, ("z", "c"), split_axis=1, concat_axis=0, tiled=True)
    rows = vec.shape[1]
    vec = vec.reshape(NZ, NC * blocks, rows, slots)
    vec = lax.all_gather(vec, "x", axis=1).reshape(total, rows, slots)

    amp = jnp.where(live, amplitudes, jnp.zeros_like(amplitudes))
    amp = lax.all_to_all(amp, "x", split_axis=1, concat_axis=0, tiled=True)
    amp = lax.all_gather(amp.reshape(NX, blocks, ROWS, slots), "y", axis=2)
    amp = lax.all_gather(amp, ("z", "c"), axis=0)
    amp = amp.reshape(NZ, NC, NX, blocks, NY * ROWS, slots)
    amp = amp.transpose(0, 2, 1, 3, 4, 5).reshape(total, NY * ROWS, slots)

    near = jnp.sum(tile_map[:, :, None] == jnp.arange(total)[None, None, :], axis=1).astype(jnp.bfloat16)
    w = jnp.einsum("qit,qkt->qik", amp, vec, preferred_element_type=jnp.float32)
    hi, lo = split(w)
    u = jnp.einsum("pq,qik->pik", near, hi, preferred_element_type=jnp.float32)
    u = u + jnp.einsum("pq,qik->pik", near, lo, preferred_element_type=jnp.float32)
    hi, lo = split(u)
    out = jnp.einsum("pik,pks->pis", hi, vec, preferred_element_type=jnp.float32)
    out = out + jnp.einsum("pik,pks->pis", lo, vec, preferred_element_type=jnp.float32)

    out = out.reshape(NZ, NX, NC, blocks, NY, ROWS, slots).transpose(4, 0, 2, 1, 3, 5, 6)
    out = lax.psum_scatter(out, "y", scatter_dimension=0)
    out = lax.psum_scatter(out.reshape((NZ * NC, NX) + out.shape[3:]), ("z", "c"), scatter_dimension=0)
    out = lax.all_to_all(out, "x", split_axis=0, concat_axis=0)
    out = out.transpose(1, 0, 2, 3).reshape(blocks, occ, slots)
    return jnp.where(live, out, 0.0).astype(jnp.bfloat16)


def solution(mesh):
    fine = Mesh(mesh.devices.reshape(NZ, NX, NC, NY), ("z", "x", "c", "y"))
    pair = ("z", "x", "c")
    return jax.shard_map(
        body,
        mesh=fine,
        in_specs=(P(pair, "y", None), P(pair, "y", None), P(pair), P()),
        out_specs=P(pair, "y", None),
        check_vma=False,
    )
```

time: 689 us -> 380 us (0.55)
  waiting for transfers between devices: 470 us -> 194 us
  blocking collectives: 11.1 us -> 87 us
  local copies, waits for them, and re-layouts: 77.7 us -> 39.2 us
  other arithmetic: 46.8 us -> 14.5 us
  starting transfers between devices: 23.6 us -> 0.13 us
  matrix products: 44.5 us -> 27.8 us
    all_to_all x2 -> x0, waiting for transfers between devices: 397 us -> none  [the longest x1 397 us: body(): lax.all_to_all(sent_vec, 'pair', split_axis=0, concat_axis=0, tiled=True)]
    reduce_scatter x1 -> x2, waiting for transfers between devices: 29.2 us -> 142 us  [the longest x1 83.8 us: body(): out = lax.psum_scatter(out, 'y', scatter_dimension=0)]
    all_to_all x0 -> x3, blocking collectives: none -> 77.1 us  [the longest x1 59.4 us: body(): lax.all_to_all(vectors, ('z', 'c'), split_axis=1, concat_axis=0, tiled=True)]
    gather x10 -> x0, local copies, waits for them, and re-layouts: 76.4 us -> none  [the longest x4 53.1 us: one_row(): partner_vec = jnp.take(pool_vec, index, axis=0)]
    concatenate x2 -> x0, other arithmetic: 23.8 us -> none  [the longest x1 19.1 us: body(): pool_vec = jnp.concatenate([masked, got_vec], axis=0)]
    all_to_all x2 -> x0, starting transfers between devices: 23.5 us -> none  [the longest x1 13 us: body(): lax.all_to_all(sent_amps, 'pair', split_axis=0, concat_axis=0, tiled=True)]
    select_n x9 -> x1, other arithmetic: 20.3 us -> 0.85 us  [body(): amp = jnp.where(live, amplitudes, jnp.zeros_like(amplitudes))]
    dot_general x8 -> x3, matrix products: 44.5 us -> 26.1 us  [the longest x1 9.84 us: body(): w = jnp.einsum('qit,qkt->qik', amp, vec, preferred_element_type=jnp.float32)]
where the time goes in v1:
time: 380 us; the launch traced here: 376 us
  waiting for transfers between devices  194 us (51%)
  blocking collectives  87 us (23%)
  local copies, waits for them, and re-layouts  39.2 us (10%)
  matrix products  27.8 us (7%)
  other arithmetic  14.5 us (4%)
  between operations  13.2 us (3%)
    reduce_scatter x1, waiting for transfers between devices, body(): out = lax.psum_scatter(out, 'y', scatter_dimension=0)  83.8 us
    all_to_all x1, blocking collectives, body(): lax.all_to_all(vectors, ('z', 'c'), split_axis=1, concat_axis=0, tiled=True)  59.4 us
    reduce_scatter x1, waiting for transfers between devices, body(): lax.psum_scatter(out.reshape((NZ * NC, NX) + out.shape[3:]), ('z', 'c'),...  58.4 us
    all_gather x1, waiting for transfers between devices, body(): vec = lax.all_gather(vec, 'x', axis=1).reshape(total, rows, slots)  51.5 us
    convert_element_type x2, local copies, waits for them, and re-layouts, split(): return (hi.astype(jnp.bfloat16), (x - hi).astype(jnp.bfloat16))  11.9 us
    all_gather x1, blocking collectives, body(): amp = lax.all_gather(amp.reshape(NX, blocks, ROWS, slots), 'y', axis=2)  9.88 us
    dot_general x1, matrix products, body(): w = jnp.einsum('qit,qkt->qik', amp, vec, preferred_element_type=jnp.float32)  9.84 us
    all_to_all x1, blocking collectives, body(): amp = lax.all_to_all(amp, 'x', split_axis=1, concat_axis=0, tiled=True)  9.12 us
  transfers between devices with their start and end apart: 4, of which 3 were waited for; matrix products, arithmetic and copies ran while one was open for 5% of the time, Pallas kernels for 0%

profile of v1, /device:TPU:1, one launch (start us, length us, event | category | flops | bytes accessed | tf_op | source)
XLA Modules:
  0.0 375.6 jit_solution(11160406354063326569)
XLA Ops:
  6.5 0.7 iota_compare_fusion.1
  7.3 0.8 broadcast_select_fusion
  8.1 0.1 copy.55
  8.2 9.1 %all_to_all.35 = bf16[4,64,128]{2,0,1:T(4,128)(2,1)S(1)} all-to-all(bf16[4,64,128]{2,0,1:T(4,128)(2,1)S(1)} %copy.55), channel_id=1, replica_groups=mesh['z'=8,'x'=4,'c'=2,'y'=4] {'x'}, dimensions={1} | all-to-all | bytes 131072 | tf_op jit(solution)/shard_map/all_to_all | solution.py:26
  17.3 9.9 %all-gather = bf16[4,4,64,128]{3,1,2,0:T(4,128)(2,1)S(1)} all-gather(bf16[4,4,16,128]{3,1,2,0:T(4,128)(2,1)S(1)} %bitcast.52), channel_id=2, replica_groups=mesh['z'=8,'x'=4,'c'=2,'y'=4] {'y'}, dimensions={2}, use_global_device_ids=true | all-gather | bytes 327680 | tf_op jit(solution)/shard_map/all_gather | solution.py:27
  27.2 0.8 copy.56
  28.0 0.0 all-gather.5.cloned.1.call-start
  28.0 6.5 %copy.58 = bf16[4,1280,128]{2,0,1:T(4,128)(2,1)S(1)} copy(bf16[4,1280,128]{2,1,0:T(8,128)(2,1)} %param.5) | data formatting | bytes 2621440 | tf_op args[1]
  34.6 59.4 %all_to_all.36 = bf16[4,1280,128]{2,0,1:T(4,128)(2,1)S(1)} all-to-all(bf16[4,1280,128]{2,0,1:T(4,128)(2,1)S(1)} %copy.58), channel_id=1, replica_groups=mesh['z'=8,'x'=4,'c'=2,'y'=4] {'z','c'}, dimensions={1} | all-to-all | bytes 2621440 | tf_op jit(solution)/shard_map/all_to_all | solution.py:20
  93.9 1.3 copy.59
  95.3 0.0 reduce-scatter.3.cloned.1.call-start
  95.3 0.1 copy.54
  95.4 5.9 %convert_reduce_fusion = s32[256,256]{1,0:T(8,128)S(1)} fusion(s32[256,32]{1,0:T(8,128)S(1)} %copy.54), kind=kLoop, calls=%fused_computation.1 | loop fusion | flops 6225920 | bytes 294912 | tf_op jit(solution)/shard_map/reduce_sum | solution.py:32
  101.3 0.0 all-gather.7.cloned.1.call-done
  101.3 5.9 %copy.57 = bf16[8,4,2,4,64,128]{5,4,3,2,1,0:T(8,128)(2,1)} copy(bf16[8,4,2,4,64,128]{5,4,3,1,2,0:T(8,128)(2,1)} %bitcast.48) | data formatting | bytes 8388608 | tf_op jit(solution)/shard_map/transpose | solution.py:30
  107.2 51.5 %all-gather.5.cloned.1.call-done = bf16[8,4,8,80,128]{4,3,2,1,0:T(8,128)(2,1)} async-done(((bf16[8,1,8,80,128]{4,3,2,1,0:T(8,128)(2,1)}), bf16[8,4,8,80,128]{4,3,2,1,0:T(8,128)(2,1)}) %all-gather.5.cloned.1.call-update) | async-done | bytes 5242896 | tf_op jit(solution)/shard_map/all_gather | solution.py:23
  158.8 9.8 %fusion.7 = f32[256,64,80]{2,1,0:T(8,128)} fusion(bf16[256,64,128]{2,1,0:T(8,128)(2,1)} %bitcast.43, bf16[256,80,128]{2,1,0:T(8,128)(2,1)} %bitcast.36), kind=kOutput, calls=%fused_computation.18 | convolution fusion | flops 335544320 | bytes 14680064 | tf_op jit(solution)/shard_map/qit,qkt->qik/dot_general | solution.py:33
  168.6 8.3 %copy.60 = f32[256,64,80]{0,2,1:T(8,128)} copy(f32[256,64,80]{2,1,0:T(8,128)} %fusion.7) | data formatting | bytes 10485760 | tf_op jit(solution)/shard_map/qit,qkt->qik/dot_general | solution.py:33
  176.9 3.3 fusion
  180.2 0.9 fusion.5
  181.1 0.9 fusion.3
  182.0 3.1 fusion.1
  185.0 6.3 %copy.62 = bf16[256,64,80]{2,1,0:T(8,128)(2,1)} copy(bf16[256,64,80]{0,2,1:T(8,128)(2,1)} %get-tuple-element.6) | data formatting | bytes 5242880 | tf_op jit(solution)/shard_map/convert_element_type | solution.py:12
  191.3 8.6 %fusion.8 = f32[256,64,128]{2,1,0:T(8,128)} fusion(bf16[256,64,80]{2,1,0:T(8,128)(2,1)} %copy.62, bf16[256,80,128]{2,1,0:T(8,128)(2,1)} %bitcast.37), kind=kOutput, calls=%fused_computation.19 | convolution fusion | flops 335544320 | bytes 16252928 | tf_op jit(solution)/shard_map/pik,pks->pis/dot_general | solution.py:38
  199.9 5.6 %copy.63 = bf16[256,64,80]{2,1,0:T(8,128)(2,1)} copy(bf16[256,64,80]{0,2,1:T(8,128)(2,1)S(1)} %get-tuple-element.5) | data formatting | bytes 5242880 | tf_op jit(solution)/shard_map/convert_element_type | solution.py:12
  205.5 7.7 %convolution_add_fusion = f32[256,64,128]{2,1,0:T(8,128)S(1)} fusion(f32[256,64,128]{2,1,0:T(8,128)} %fusion.8, bf16[256,64,80]{2,1,0:T(8,128)(2,1)} %copy.63, bf16[256,80,128]{2,1,0:T(8,128)(2,1)} %bitcast.38), kind=kOutput, calls=%fused_computation.9 | convolution fusion | flops 337641472 | bytes 24641536 | tf_op jit(solution)/shard_map/pik,pks->pis/dot_general | solution.py:39
  213.2 4.3 %copy.67 = f32[8,4,2,4,4,16,128]{6,5,3,1,2,0,4:T(8,128)} copy(f32[8,4,2,4,4,16,128]{6,5,4,3,2,1,0:T(8,128)S(1)} %bitcast.39) | data formatting | bytes 16777216 | tf_op jit(solution)/shard_map/reshape | solution.py:41
  217.5 0.0 reduce-scatter.5.cloned.1.call-start
  217.6 83.8 %reduce-scatter.3.cloned.1.call-done = f32[1,8,2,4,4,16,128]{6,5,4,3,2,1,0:T(8,128)} async-done(((f32[4,8,2,4,4,16,128]{6,5,4,3,2,1,0:T(8,128)}), f32[1,8,2,4,4,16,128]{6,5,4,3,2,1,0:T(8,128)}) %reduce-scatter.3.cloned.1.call-update) | async-done | bytes 2097168 | tf_op jit(solution)/shard_map/reduce_scatter | solution.py:42
  301.4 58.4 %reduce-scatter.5.cloned.1.call-done = f32[1,4,4,16,128]{4,3,2,1,0:T(8,128)} async-done(((f32[16,4,4,16,128]{4,3,2,1,0:T(8,128)}), f32[1,4,4,16,128]{4,3,2,1,0:T(8,128)}) %reduce-scatter.5.cloned.1.call-update) | async-done | bytes 131088 | tf_op jit(solution)/shard_map/reduce_scatter | solution.py:43
  359.8 8.6 %all_to_all.37 = f32[4,4,16,128]{3,2,1,0:T(8,128)S(1)} all-to-all(f32[4,4,16,128]{3,2,1,0:T(8,128)} %bitcast.53), channel_id=1, replica_groups=mesh['z'=8,'x'=4,'c'=2,'y'=4] {'x'}, dimensions={0} | all-to-all | bytes 262144 | tf_op jit(solution)/shard_map/all_to_all | solution.py:44
  368.4 0.7 fusion.2
  (8 shorter events, 0.1 us)
Async XLA Ops:
  6.5 94.8 %all-gather.7.cloned.1.call-start = ((), (), s32[]{:S(2)}) async-start(), calls=%async_computation.8 | async-start | bytes 4456448 | tf_op jit(solution)/shard_map/all_gather | solution.py:28
  8.2 87.2 %copy-start = (s32[256,32]{0,1:T(8,128)S(1)}, s32[256,32]{0,1:T(8,128)}, u32[]{:S(2)}) copy-start(s32[256,32]{0,1:T(8,128)} %param.7) | copy-start | bytes 98308
  28.0 130.8 %all-gather.5.cloned.1.call-start = ((), (), s32[]{:S(2)}) async-start(), calls=%async_computation.5 | async-start | bytes 6553600 | tf_op jit(solution)/shard_map/all_gather | solution.py:23
  95.3 206.1 %reduce-scatter.3.cloned.1.call-start = ((), (), s32[]{:S(2)}) async-start(), calls=%async_computation.6 | async-start | bytes 10485760 | tf_op jit(solution)/shard_map/reduce_scatter | solution.py:42
  217.5 142.3 %reduce-scatter.5.cloned.1.call-start = ((), (), s32[]{:S(2)}) async-start(), calls=%async_computation.7 | async-start | bytes 2228224 | tf_op jit(solution)/shard_map/reduce_scatter | solution.py:43
Sparse Core Ops, SparseCore 0:
  28.1 71.4 all-gather.6
  101.4 57.3 all-gather.4
  217.6 83.6 reduce-scatter.2
  303.8 56.0 reduce-scatter.4

commit v2 on v1

v2 whole, which is shorter than its diff:
```python
import jax
import jax.numpy as jnp
from jax import lax
from jax.experimental import pallas as pl
from jax.experimental.pallas import tpu as pltpu
from jax.sharding import Mesh, PartitionSpec as P

NZ, NX, NC, NY = 8, 4, 2, 4
BLOCKS = 4
GROUP = NX * NC * BLOCKS
TOTAL = NZ * GROUP
SLOTS = 128
DEPTH = 160
ROWS = 16
PITCH = TOTAL + 8
FIRST = 20
REST = GROUP - FIRST


def split(x):
    hi = x.astype(jnp.bfloat16)
    return hi, (x - hi.astype(jnp.float32)).astype(jnp.bfloat16)


def wait(view, sem):
    pltpu.make_async_copy(view, view, sem).wait()


def kernel(
    amp, vec, near, out,
    vb, ab, w, o, gzb, fzb, yhf, yff, yhg, yfg, fb, fr,
    vzs, vzr, xs, xr, ss, sr, axs, axr, azs, azr, ays, ayr,
    gzs, gzr, fzs, fzr, yhs, yhr, yfs, yfr, es, er,
):
    z, x, c, y = (lax.axis_index(a) for a in ("z", "x", "c", "y"))

    def mod(a, n):
        return lax.rem(a + 4 * n, n)

    def send(src, dst, ssem, rsem, z1=z, x1=x, c1=c, y1=y):
        pltpu.make_async_remote_copy(
            src_ref=src, dst_ref=dst, send_sem=ssem, recv_sem=rsem,
            device_id=(z1, x1, c1, y1), device_id_type=pl.DeviceIdType.MESH,
        ).start()

    zp, zm = mod(z + 1, NZ), mod(z - 1, NZ)
    xp, xm, xo = mod(x + 1, NX), mod(x - 1, NX), mod(x + 2, NX)
    yp, ym = mod(y + 1, NY), mod(y - 1, NY)
    mate = 1 - c
    home, edge = lax.div(y, 2), lax.rem(y, 2)
    active = c == home

    def mine(x0, c0):
        return pl.ds(pl.multiple_of(x0 * (NC * BLOCKS) + c0 * BLOCKS, BLOCKS), BLOCKS)

    def part(x0, c0, h):
        return pl.ds(x0 * (NC * BLOCKS) + c0 * BLOCKS + 2 * h, 2)

    def rows(z1):
        return pl.ds(pl.multiple_of(z1 * DEPTH, DEPTH), DEPTH)

    own = pltpu.make_async_copy(vec.at[:, rows(z), :], vb.at[z, mine(x, c)], vzr.at[z])
    own.start()
    barrier = pltpu.get_barrier_semaphore()

    def greet(z1=z, x1=x, c1=c, y1=y):
        pl.semaphore_signal(barrier, inc=1, device_id=(z1, x1, c1, y1), device_id_type=pl.DeviceIdType.MESH)

    for d in range(1, NZ):
        greet(z1=mod(z + d, NZ))
    for d in range(NX):
        for e in range(NC):
            if d or e:
                greet(x1=mod(x + d, NX), c1=mod(c + e, NC))
    for d in range(1, NY):
        greet(y1=mod(y + d, NY))
    pl.semaphore_wait(barrier, NZ - 1 + NX * NC - 1 + NY - 1)

    for d in range(NX):
        x1 = mod(x + d, NX)
        src = amp.at[:, pl.ds(pl.multiple_of(x1 * ROWS, ROWS), ROWS), :]
        dst = ab.at[edge, z, mine(x, c)]
        if d:
            send(src, dst, axs.at[d], axr.at[x, c], x1=x1, c1=home)
        else:

            @pl.when(active)
            def _():
                pltpu.make_async_copy(src, dst, axr.at[x, c]).start()

            @pl.when(c != home)
            def _():
                send(src, dst, axs.at[0], axr.at[x, c], c1=home)

    for d in (1, -1, 2, -2, 3, -3, 4):
        z1 = mod(z + d, NZ)
        send(vec.at[:, rows(z1), :], vb.at[z, mine(x, c)], vzs.at[z1], vzr.at[z], z1=z1)

    def source(s):
        return mod(z - jnp.where(lax.rem(s, 2) == 1, lax.div(s + 1, 2), -lax.div(s, 2)), NZ)

    def spread_amp(z0):
        for d in range(1, NY):
            send(ab.at[edge, z0], ab.at[edge, z0], ays.at[d - 1, z0], ayr.at[edge, z0], y1=mod(y + d, NY))

    def products(z0):
        for e in range(2):

            @pl.when(y != 2 * c + e)
            def _():
                wait(ab.at[e, z0], ayr.at[e, z0])

        def some(n, carry):
            for u in range(4):
                q = n * 4 + u
                a = jnp.concatenate([ab[0, z0, q], ab[1, z0, q]], axis=0)
                r = lax.dot_general(a, vb[z0, q], (((1,), (1,)), ((), ())), preferred_element_type=jnp.float32)
                w[0, pl.ds(z0 * GROUP + q, 2 * ROWS, stride=PITCH), :] = r[:, :SLOTS]
                w[1, pl.ds(z0 * GROUP + q, 2 * ROWS, stride=PITCH), : DEPTH - SLOTS] = r[:, SLOTS:]
            return carry

        lax.fori_loop(0, GROUP // 4, some, 0)

    def step(s, carry):
        @pl.when(s < NZ)
        def _():
            z0 = source(s)
            block = vb.at[z0, mine(x, c)]
            wait(block, vzr.at[z0])
            send(block, block, xs.at[0, z0], xr.at[0, z0], x1=xp)
            send(block, block, xs.at[1, z0], xr.at[1, z0], x1=xm)
            send(block, block, ss.at[0, z0], sr.at[0, z0], c1=mate)

        @pl.when(jnp.logical_and(s >= 1, s < NZ + 1))
        def _():
            z0 = source(s - 1)
            left, right = vb.at[z0, mine(xm, c)], vb.at[z0, mine(xp, c)]
            wait(left, xr.at[0, z0])
            half = vb.at[z0, part(xm, c, 0)]
            send(half, half, xs.at[2, z0], xr.at[2, z0], x1=xp)
            send(left, left, ss.at[1, z0], sr.at[1, z0], c1=mate)
            wait(right, xr.at[1, z0])
            half = vb.at[z0, part(xp, c, 1)]
            send(half, half, xs.at[3, z0], xr.at[3, z0], x1=xm)
            send(right, right, ss.at[2, z0], sr.at[2, z0], c1=mate)

        @pl.when(jnp.logical_and(s == 0, active))
        def _():
            for x0 in range(NX):
                for c0 in range(NC):
                    wait(ab.at[edge, z, mine(x0, c0)], axr.at[x0, c0])
            spread_amp(z)
            for d in (1, -1, 2, -2, 3, -3, 4):
                z1 = mod(z + d, NZ)
                send(ab.at[edge, z], ab.at[edge, z], azs.at[z1], azr.at[z], z1=z1)

        @pl.when(jnp.logical_and(jnp.logical_and(s >= 1, s < NZ), active))
        def _():
            z0 = source(s)
            wait(ab.at[edge, z0], azr.at[z0])
            spread_amp(z0)

        @pl.when(jnp.logical_and(s >= 2, s < NZ + 2))
        def _():
            z0 = source(s - 2)
            wait(vb.at[z0, part(xo, c, 0)], xr.at[2, z0])
            wait(vb.at[z0, part(xo, c, 1)], xr.at[3, z0])
            block = vb.at[z0, mine(xo, c)]
            send(block, block, ss.at[3, z0], sr.at[3, z0], c1=mate)

        @pl.when(s >= 3)
        def _():
            z0 = source(s - 3)
            for k, x0 in enumerate((x, xm, xp, xo)):
                wait(vb.at[z0, mine(x0, mate)], sr.at[k, z0])
            products(z0)

        return carry

    lax.fori_loop(0, NZ + 3, step, 0)

    def mix(i, carry):
        at = pl.ds(pl.multiple_of(i * PITCH, 8), TOTAL)
        for h in range(2):
            hi, lo = split(w[h, at, :])
            u = jnp.dot(near[...], hi, preferred_element_type=jnp.float32)
            w[h, at, :] = u + jnp.dot(near[...], lo, preferred_element_type=jnp.float32)
        return carry

    lax.fori_loop(0, 2 * ROWS, mix, 0)

    def residuals(zt):
        def some(n, carry):
            for u in range(4):
                p = n * 4 + u
                at = pl.ds(zt * GROUP + p, 2 * ROWS, stride=PITCH)
                hi0, lo0 = split(w[0, at, :])
                hi1, lo1 = split(w[1, at, :])
                left = jnp.concatenate([hi0, lo0], axis=0)
                right = jnp.concatenate([hi1, lo1], axis=0)[:, : DEPTH - SLOTS]
                r = jnp.dot(left, vb[zt, p, :SLOTS, :], preferred_element_type=jnp.float32)
                r = r + jnp.dot(right, vb[zt, p, SLOTS:, :], preferred_element_type=jnp.float32)
                r = r[: 2 * ROWS] + r[2 * ROWS :]
                o[0, zt, p] = r[:ROWS]
                o[1, zt, p] = r[ROWS:]
            return carry

        lax.fori_loop(0, GROUP // 4, some, 0)

    around = mod(y - 2 * c, NY)
    near_e, other_e = 1 - lax.rem(around, 2), lax.rem(around, 2)
    behind = jnp.logical_or(around == 0, around == 3)
    side = jnp.where(behind, 1, 0)
    onward = jnp.where(behind, yp, ym)

    def span(n):
        return (0, FIRST, yhf.at[n], yff.at[:, n]) if n < NZ else (FIRST, REST, yhg, yfg)

    def y1(n, zt):
        lo, size, hb, _ = span(n)

        @pl.when(jnp.logical_not(active))
        def _():
            send(o.at[other_e, zt, pl.ds(lo, size // 2)], hb, yhs.at[0, n], yhr.at[n], y1=ym)
            send(o.at[other_e, zt, pl.ds(lo + size // 2, size // 2)], hb, yhs.at[1, n], yhr.at[n], y1=yp)

    def y2(n, zt):
        lo, size, hb, fb_ = span(n)
        wait(hb, yhr.at[n])
        at = pl.ds(lo + side * (size // 2), size // 2)
        o[near_e, zt, at] = o[near_e, zt, at] + hb[...]
        send(o.at[near_e, zt, pl.ds(lo, size)], fb_.at[side], yfs.at[n], yfr.at[side, n], y1=onward)

    def y3(n, zt):
        lo, size, _, fb_ = span(n)

        @pl.when(active)
        def _():
            for k in range(2):
                wait(fb_.at[k], yfr.at[k, n])
            at = pl.ds(lo, size)
            o[other_e, zt, at] = o[other_e, zt, at] + (fb_[0] + fb_[1])

    def gview(zt, t, k):
        return o.at[pl.ds(k, 1), zt, pl.ds(FIRST, REST)] if t == 0 else o.at[:, zt, pl.ds(FIRST, REST)]

    def fview(zt, t, k):
        return o.at[other_e, zt, pl.ds(k * (FIRST // 2), FIRST // 2)] if t == 0 else o.at[other_e, zt, pl.ds(0, FIRST)]

    def gland(t, k):
        return gzb.at[k, t, pl.ds(0, 1)] if t == 0 else gzb.at[k, t]

    def fland(t, k):
        return fzb.at[k, t, pl.ds(0, FIRST // 2)] if t == 0 else fzb.at[k, t]

    def zsend(view, land, ssem, rsem, k, t):
        zt = mod(z + (4 - t), NZ) if k == 0 else mod(z - (4 - t), NZ)
        send(view(zt, t, k), land(t, k), ssem.at[k, t], rsem.at[k, t], z1=zp if k == 0 else zm)

    def zrecv(view, land, rsem, k, t):
        zt = mod(z + (3 - t), NZ) if k == 0 else mod(z - (3 - t), NZ)
        wait(land(t, k), rsem.at[k, t])
        into = view(zt, t, k)
        into[...] = into[...] + land(t, k)[...]

    def zwork(m, view, land, ssem, rsem):
        if m == 0:
            for k in range(2):
                zsend(view, land, ssem, rsem, k, 0)
        elif m < 7:
            k, t = (0, (m - 1) // 2) if m % 2 else (1, m // 2 - 1)
            zrecv(view, land, rsem, k, t)
            zsend(view, land, ssem, rsem, k, t + 1)
        else:
            for k in range(2):
                zrecv(view, land, rsem, k, 3)

    def g(m):
        zwork(m, gview, gland, gzs, gzr)

    def f(m):
        @pl.when(active)
        def _():
            zwork(m, fview, fland, fzs, fzr)

    order = [mod(z + d, NZ) for d in (4, 3, -3, 2, -2, 1, -1, 0)]
    for n in range(NZ):
        residuals(order[n])
        y1(n, order[n])
        if n >= 1:
            y2(n - 1, order[n - 1])
        if n < 7:
            g(n)
        if n >= 2:
            y3(n - 2, order[n - 2])
            f(n - 2)
    y2(7, z)
    y3(6, order[6])
    f(6)
    g(7)
    y1(8, z)
    y3(7, z)
    y2(8, z)
    f(7)
    y3(8, z)

    @pl.when(active)
    def _():
        fb[...] = o[other_e, z].astype(jnp.bfloat16)
        for d in range(NX):
            for e in range(NC):
                x1, c1 = mod(x + d, NX), mod(c + e, NC)
                src = fb.at[mine(x1, c1)]
                dst = fr.at[:, pl.ds(pl.multiple_of(x * ROWS, ROWS), ROWS), :]
                if d or e:
                    send(src, dst, es.at[2 * d + e], er.at[x], x1=x1, c1=c1)
                else:
                    pltpu.make_async_copy(src, dst, er.at[x]).start()

    for x0 in range(NX):
        wait(fr.at[:, pl.ds(x0 * ROWS, ROWS), :], er.at[x0])
    out[...] = fr[...]

    piece = amp.at[:, pl.ds(0, ROWS), :]
    for d in range(1, NX):
        wait(piece, axs.at[d])

    @pl.when(c != home)
    def _():
        wait(piece, axs.at[0])

    def sent(n, carry):
        z0 = mod(z + n, NZ)
        block, half = vb.at[z0, mine(x, c)], vb.at[z0, part(x, c, 0)]
        for k in range(2):
            wait(block, xs.at[k, z0])
            wait(half, xs.at[2 + k, z0])
        for k in range(4):
            wait(block, ss.at[k, z0])

        @pl.when(n > 0)
        def _():
            wait(block, vzs.at[z0])

        @pl.when(active)
        def _():
            for k in range(NY - 1):
                wait(ab.at[edge, z0], ays.at[k, z0])

            @pl.when(n > 0)
            def _():
                wait(ab.at[edge, z0], azs.at[z0])

        return carry

    lax.fori_loop(0, NZ, sent, 0)
    for n in range(NZ + 1):
        lo, size, hb, fb_ = span(n)

        @pl.when(jnp.logical_not(active))
        def _():
            wait(hb, yhs.at[0, n])
            wait(hb, yhs.at[1, n])

        wait(fb_.at[0], yfs.at[n])
    for k in range(2):
        for t in range(4):
            wait(gland(t, k), gzs.at[k, t])

    @pl.when(active)
    def _():
        for k in range(2):
            for t in range(4):
                wait(fland(t, k), fzs.at[k, t])
        for n in range(1, NX * NC):
            wait(fb.at[pl.ds(0, BLOCKS)], es.at[n])


def body(amplitudes, vectors, pair_count, tile_map):
    live = lax.broadcasted_iota(jnp.int32, (BLOCKS, 1, SLOTS), 2) < pair_count[:, None, None]
    amp = jnp.where(live, amplitudes, jnp.zeros_like(amplitudes))
    near = jnp.sum(tile_map[:, :, None] == jnp.arange(TOTAL)[None, None, :], axis=1).astype(jnp.bfloat16)
    f32, bf16 = jnp.float32, jnp.bfloat16
    dma = pltpu.SemaphoreType.DMA
    out = pl.pallas_call(
        kernel,
        out_shape=jax.ShapeDtypeStruct(amplitudes.shape, bf16),
        in_specs=[
            pl.BlockSpec(memory_space=pltpu.VMEM),
            pl.BlockSpec(memory_space=pl.ANY),
            pl.BlockSpec(memory_space=pltpu.VMEM),
        ],
        out_specs=pl.BlockSpec(memory_space=pltpu.VMEM),
        scratch_shapes=[
            pltpu.VMEM((NZ, GROUP, DEPTH, SLOTS), bf16),
            pltpu.VMEM((2, NZ, GROUP, ROWS, SLOTS), bf16),
            pltpu.VMEM((2, 2 * ROWS * PITCH, SLOTS), f32),
            pltpu.VMEM((2, NZ, GROUP, ROWS, SLOTS), f32),
            pltpu.VMEM((2, 4, 2, REST, ROWS, SLOTS), f32),
            pltpu.VMEM((2, 4, FIRST, ROWS, SLOTS), f32),
            pltpu.VMEM((NZ, FIRST // 2, ROWS, SLOTS), f32),
            pltpu.VMEM((2, NZ, FIRST, ROWS, SLOTS), f32),
            pltpu.VMEM((REST // 2, ROWS, SLOTS), f32),
            pltpu.VMEM((2, REST, ROWS, SLOTS), f32),
            pltpu.VMEM((GROUP, ROWS, SLOTS), bf16),
            pltpu.VMEM((BLOCKS, NX * ROWS, SLOTS), bf16),
            dma((NZ,)), dma((NZ,)),
            dma((4, NZ)), dma((4, NZ)),
            dma((4, NZ)), dma((4, NZ)),
            dma((NX,)), dma((NX, NC)),
            dma((NZ,)), dma((NZ,)),
            dma((NY - 1, NZ)), dma((2, NZ)),
            dma((2, 4)), dma((2, 4)),
            dma((2, 4)), dma((2, 4)),
            dma((2, NZ + 1)), dma((NZ + 1,)),
            dma((NZ + 1,)), dma((2, NZ + 1)),
            dma((NX * NC,)), dma((NX,)),
        ],
        compiler_params=pltpu.CompilerParams(
            collective_id=0, has_side_effects=True, vmem_limit_bytes=60 * 2**20
        ),
        cost_estimate=pl.CostEstimate(flops=12 * 10**9, bytes_accessed=4 * 10**6, transcendentals=0),
    )(amp, vectors, near)
    return jnp.where(live, out, jnp.zeros_like(out))


def solution(mesh):
    fine = Mesh(mesh.devices.reshape(NZ, NX, NC, NY), ("z", "x", "c", "y"))
    pair = ("z", "x", "c")
    return jax.shard_map(
        body,
        mesh=fine,
        in_specs=(P(pair, "y", None), P(pair, "y", None), P(pair), P()),
        out_specs=P(pair, "y", None),
        check_vma=False,
    )
```

time: 380 us -> 141 us (0.37)
  waiting for transfers between devices: 194 us -> 0 us
  Pallas kernels: 0 us -> 129 us
  blocking collectives: 87 us -> 0 us
  local copies, waits for them, and re-layouts: 39.2 us -> 0.85 us
  matrix products: 27.8 us -> 0 us
  between operations: 13.2 us -> 0.01 us
  other arithmetic: 14.5 us -> 10 us
    reduce_scatter x2 -> x0, waiting for transfers between devices: 142 us -> none  [the longest x1 83.8 us: body(): out = lax.psum_scatter(out, 'y', scatter_dimension=0)]
    pallas_call x0 -> x1, Pallas kernels: none -> 129 us  [body(): pl.pallas_call(kernel, out_shape=jax.ShapeDtypeStruct(amplitudes.shape, b...]
    all_to_all x3 -> x0, blocking collectives: 77.1 us -> none  [the longest x1 59.4 us: body(): lax.all_to_all(vectors, ('z', 'c'), split_axis=1, concat_axis=0, tiled=True)]
    all_gather x2 -> x0, waiting for transfers between devices: 51.6 us -> none  [the longest x1 51.5 us: body(): vec = lax.all_gather(vec, 'x', axis=1).reshape(total, rows, slots)]
    dot_general x3 -> x0, matrix products: 26.1 us -> none  [the longest x1 9.84 us: body(): w = jnp.einsum('qit,qkt->qik', amp, vec, preferred_element_type=jnp.float32)]
    convert_element_type x2 -> x0, local copies, waits for them, and re-layouts: 11.9 us -> none  [split(): return (hi.astype(jnp.bfloat16), (x - hi).astype(jnp.bfloat16))]
    all_gather x1 -> x0, blocking collectives: 9.88 us -> none  [body(): amp = lax.all_gather(amp.reshape(NX, blocks, ROWS, slots), 'y', axis=2)]
    dot_general x1 -> x0, local copies, waits for them, and re-layouts: 8.29 us -> none  [body(): w = jnp.einsum('qit,qkt->qik', amp, vec, preferred_element_type=jnp.float32)]
  transfers between devices with their start and end apart: 4 -> 0, of which waited for: 3 -> 0; matrix products, arithmetic and copies ran while one was open for 5% -> 0% of each run, Pallas kernels for 0% -> 0%
where the time goes in v2:
time: 141 us; the launch traced here: 140 us
  Pallas kernels  129 us (91%)
  other arithmetic  10 us (7%)
    pallas_call x1, Pallas kernels, body(): pl.pallas_call(kernel, out_shape=jax.ShapeDtypeStruct(amplitudes.shape, b...  129 us
    reduce_sum x1, other arithmetic, body(): jnp.sum(tile_map[:, :, None] == jnp.arange(TOTAL)[None, None, :], axis=1)  5.69 us

profile of v2, /device:TPU:1, one launch (start us, length us, event | category | flops | bytes accessed | tf_op | source)
XLA Modules:
  0.0 140.4 jit_solution(17471362421520258558)
XLA Ops:
  0.0 0.7 iota_compare_fusion.1
  0.7 1.5 %broadcast_select_fusion.1.amp = bf16[4,64,128]{2,1,0:T(8,128)(2,1)} fusion(bf16[4,64,128]{2,1,0:T(8,128)(2,1)} %param.4, pred[4,128]{1,0:T(4,128)(4,1)S(1)} %iota_compare_fusion.1), kind=kLoop, calls=%fused_computation.3 | loop fusion | flops 32768 | bytes 131584 | tf_op jit(solution)/shard_map/jit(_where)/select_n | solution.py:381
  2.2 0.9 copy.6
  3.1 5.7 %convert_reduce_fusion = s32[256,256]{1,0:T(8,128)S(1)} fusion(s32[256,32]{1,0:T(8,128)S(1)} %copy.6), kind=kLoop, calls=%fused_computation | loop fusion | flops 6225920 | bytes 294912 | tf_op jit(solution)/shard_map/reduce_sum | solution.py:382
  8.7 0.7 convert_element_type.7.near
  9.4 129.5 %shard_map.46 = bf16[4,64,128]{2,1,0:T(8,128)(2,1)} custom-call(bf16[4,64,128]{2,1,0:T(8,128)(2,1)} %broadcast_select_fusion.1.amp, bf16[4,1280,128]{2,1,0:T(8,128)(2,1)} %vec.1, bf16[256,256]{1,0:T(8,128)(2,1)} %convert_element_type.7.near), custom_call_target="tpu_custom_call" | custom-call | flops 12000000000 | bytes 4000000 | tf_op jit(solution)/shard_map/pallas_call | solution.py:385
  138.9 1.5 %broadcast_select_fusion = bf16[4,64,128]{2,1,0:T(8,128)(2,1)} fusion(bf16[4,64,128]{2,1,0:T(8,128)(2,1)} %shard_map.46, pred[4,128]{1,0:T(4,128)(4,1)S(1)} %iota_compare_fusion.1), kind=kLoop, calls=%fused_computation.2 | loop fusion | flops 32768 | bytes 131584 | tf_op jit(solution)/shard_map/jit(_where)/select_n | solution.py:424

commit v3 on v2

--- a/solution.py
+++ b/solution.py
@@ -13,6 +13,7 @@
 DEPTH = 160
 ROWS = 16
 PITCH = TOTAL + 8
+FOLD = SLOTS // (DEPTH - SLOTS)
 FIRST = 20
 REST = GROUP - FIRST
 
@@ -27,9 +28,9 @@
 
 
 def kernel(
-    amp, vec, near, out,
-    vb, ab, w, o, gzb, fzb, yhf, yff, yhg, yfg, fb, fr,
-    vzs, vzr, xs, xr, ss, sr, axs, axr, azs, azr, ays, ayr,
+    amp_in, vec, counts, tiles, out,
+    amp, near, vb, ab, w, wt, o, gzb, fzb, yhf, yff, yhg, yfg, fb, fr,
+    vzs, vzr, xs, xr, ss, sr, axs, axr, azs, azr, ays, ayf, ayr,
     gzs, gzr, fzs, fzr, yhs, yhr, yfs, yfr, es, er,
 ):
     z, x, c, y = (lax.axis_index(a) for a in ("z", "x", "c", "y"))
@@ -62,6 +63,7 @@
     own = pltpu.make_async_copy(vec.at[:, rows(z), :], vb.at[z, mine(x, c)], vzr.at[z])
     own.start()
     barrier = pltpu.get_barrier_semaphore()
+    slot = lax.broadcasted_iota(jnp.int32, (NX * ROWS, SLOTS), 1)
 
     def greet(z1=z, x1=x, c1=c, y1=y):
         pl.semaphore_signal(barrier, inc=1, device_id=(z1, x1, c1, y1), device_id_type=pl.DeviceIdType.MESH)
@@ -74,6 +76,8 @@
                 greet(x1=mod(x + d, NX), c1=mod(c + e, NC))
     for d in range(1, NY):
         greet(y1=mod(y + d, NY))
+    for b in range(BLOCKS):
+        amp[b] = jnp.where(slot < counts[b], amp_in[b], jnp.zeros_like(amp_in[b]))
     pl.semaphore_wait(barrier, NZ - 1 + NX * NC - 1 + NY - 1)
 
     for d in range(NX):
@@ -99,27 +103,50 @@
     def source(s):
         return mod(z - jnp.where(lax.rem(s, 2) == 1, lax.div(s + 1, 2), -lax.div(s, 2)), NZ)
 
+    around = mod(y - 2 * c, NY)
+    near_e, other_e = 1 - lax.rem(around, 2), lax.rem(around, 2)
+    behind = jnp.logical_or(around == 0, around == 3)
+    side = jnp.where(behind, 1, 0)
+    onward, away = jnp.where(behind, yp, ym), jnp.where(behind, ym, yp)
+
+    def amp_half(h):
+        return pl.ds(pl.multiple_of(h * (GROUP // 2), GROUP // 2), GROUP // 2)
+
     def spread_amp(z0):
-        for d in range(1, NY):
-            send(ab.at[edge, z0], ab.at[edge, z0], ays.at[d - 1, z0], ayr.at[edge, z0], y1=mod(y + d, NY))
+        block = ab.at[other_e, z0]
+        send(block, block, ays.at[0, z0], ayr.at[0, z0], y1=yp)
+        send(block, block, ays.at[1, z0], ayr.at[0, z0], y1=ym)
 
     def products(z0):
-        for e in range(2):
-
-            @pl.when(y != 2 * c + e)
-            def _():
-                wait(ab.at[e, z0], ayr.at[e, z0])
+        @pl.when(jnp.logical_not(active))
+        def _():
+            for h in range(2):
+                wait(ab.at[other_e, z0, amp_half(h)], ayr.at[1 + h, z0])
 
         def some(n, carry):
             for u in range(4):
                 q = n * 4 + u
                 a = jnp.concatenate([ab[0, z0, q], ab[1, z0, q]], axis=0)
                 r = lax.dot_general(a, vb[z0, q], (((1,), (1,)), ((), ())), preferred_element_type=jnp.float32)
-                w[0, pl.ds(z0 * GROUP + q, 2 * ROWS, stride=PITCH), :] = r[:, :SLOTS]
-                w[1, pl.ds(z0 * GROUP + q, 2 * ROWS, stride=PITCH), : DEPTH - SLOTS] = r[:, SLOTS:]
+                w[pl.ds(z0 * GROUP + q, 2 * ROWS, stride=PITCH), :] = r[:, :SLOTS]
+                tail = [r[m * 8 : m * 8 + 8, SLOTS:] for m in range(FOLD)]
+                wt[pl.ds(z0 * GROUP + q, 8, stride=PITCH), :] = jnp.concatenate(tail, axis=1)
             return carry
 
         lax.fori_loop(0, GROUP // 4, some, 0)
+
+    def adjacency(n, carry):
+        at = pl.ds(pl.multiple_of(n * 32, 32), 32)
+        named = tiles[at, :]
+        block = lax.broadcasted_iota(jnp.int32, (32, TOTAL), 1)
+        found = jnp.zeros((32, TOTAL), jnp.float32)
+        for j in range(tiles.shape[1]):
+            found = found + jnp.where(named[:, j : j + 1] == block, 1.0, 0.0)
+        near[at, :TOTAL] = found.astype(jnp.bfloat16)
+        near[at, TOTAL:] = found.astype(jnp.bfloat16)
+        return carry
+
+    lax.fori_loop(0, TOTAL // 32, adjacency, 0)
 
     def step(s, carry):
         @pl.when(s < NZ)
@@ -149,16 +176,29 @@
             for x0 in range(NX):
                 for c0 in range(NC):
                     wait(ab.at[edge, z, mine(x0, c0)], axr.at[x0, c0])
+            block = ab.at[edge, z]
+            send(block, block, azs.at[z], azr.at[z], z1=zp)
+            send(block, block, azs.at[NZ], azr.at[z], z1=zm)
             spread_amp(z)
-            for d in (1, -1, 2, -2, 3, -3, 4):
-                z1 = mod(z + d, NZ)
-                send(ab.at[edge, z], ab.at[edge, z], azs.at[z1], azr.at[z], z1=z1)
 
         @pl.when(jnp.logical_and(jnp.logical_and(s >= 1, s < NZ), active))
         def _():
             z0 = source(s)
-            wait(ab.at[edge, z0], azr.at[z0])
+            block = ab.at[edge, z0]
+            wait(block, azr.at[z0])
+
+            @pl.when(s < NZ - 2)
+            def _():
+                send(block, block, azs.at[z0], azr.at[z0], z1=jnp.where(lax.rem(s, 2) == 1, zp, zm))
+
             spread_amp(z0)
+
+        @pl.when(jnp.logical_and(s >= 1, s < NZ + 1))
+        def _():
+            z0 = source(s - 1)
+            wait(ab.at[near_e, z0], ayr.at[0, z0])
+            half = ab.at[near_e, z0, amp_half(side)]
+            send(half, half, ayf.at[z0], ayr.at[1 + side, z0], y1=away)
 
         @pl.when(jnp.logical_and(s >= 2, s < NZ + 2))
         def _():
@@ -179,39 +219,39 @@
 
     lax.fori_loop(0, NZ + 3, step, 0)
 
-    def mix(i, carry):
-        at = pl.ds(pl.multiple_of(i * PITCH, 8), TOTAL)
-        for h in range(2):
-            hi, lo = split(w[h, at, :])
-            u = jnp.dot(near[...], hi, preferred_element_type=jnp.float32)
-            w[h, at, :] = u + jnp.dot(near[...], lo, preferred_element_type=jnp.float32)
-        return carry
-
-    lax.fori_loop(0, 2 * ROWS, mix, 0)
+    def mix(ref):
+        def some(i, carry):
+            at = [pl.ds(pl.multiple_of((2 * i + h) * PITCH, 8), TOTAL) for h in range(2)]
+            hi, lo = split(jnp.concatenate([ref[a, :] for a in at], axis=1))
+            u = jnp.dot(near[...], jnp.concatenate([hi, lo], axis=0), preferred_element_type=jnp.float32)
+            for h in range(2):
+                ref[at[h], :] = u[:, h * SLOTS : (h + 1) * SLOTS]
+            return carry
+
+        lax.fori_loop(0, ref.shape[0] // PITCH // 2, some, 0)
+
+    mix(w)
+    mix(wt)
+    row = lax.broadcasted_iota(jnp.int32, (2 * ROWS, SLOTS), 0)
+    lane = lax.broadcasted_iota(jnp.int32, (2 * ROWS, SLOTS), 1)
+    own_fold = lax.div(row, 8) == lax.div(lane, DEPTH - SLOTS)
 
     def residuals(zt):
         def some(n, carry):
             for u in range(4):
                 p = n * 4 + u
-                at = pl.ds(zt * GROUP + p, 2 * ROWS, stride=PITCH)
-                hi0, lo0 = split(w[0, at, :])
-                hi1, lo1 = split(w[1, at, :])
-                left = jnp.concatenate([hi0, lo0], axis=0)
-                right = jnp.concatenate([hi1, lo1], axis=0)[:, : DEPTH - SLOTS]
-                r = jnp.dot(left, vb[zt, p, :SLOTS, :], preferred_element_type=jnp.float32)
-                r = r + jnp.dot(right, vb[zt, p, SLOTS:, :], preferred_element_type=jnp.float32)
+                full = w[pl.ds(zt * GROUP + p, 2 * ROWS, stride=PITCH), :]
+                tail = jnp.concatenate([wt[pl.ds(zt * GROUP + p, 8, stride=PITCH), :]] * FOLD, axis=0)
+                u2 = jnp.concatenate([full, jnp.where(own_fold, tail, 0.0)], axis=1)
+                left = jnp.concatenate(split(u2), axis=0)
+                right = jnp.concatenate([vb[zt, p, :SLOTS, :]] + [vb[zt, p, SLOTS:, :]] * FOLD, axis=0)
+                r = jnp.dot(left, right, preferred_element_type=jnp.float32)
                 r = r[: 2 * ROWS] + r[2 * ROWS :]
                 o[0, zt, p] = r[:ROWS]
                 o[1, zt, p] = r[ROWS:]
             return carry
 
         lax.fori_loop(0, GROUP // 4, some, 0)
-
-    around = mod(y - 2 * c, NY)
-    near_e, other_e = 1 - lax.rem(around, 2), lax.rem(around, 2)
-    behind = jnp.logical_or(around == 0, around == 3)
-    side = jnp.where(behind, 1, 0)
-    onward = jnp.where(behind, yp, ym)
 
     def span(n):
         return (0, FIRST, yhf.at[n], yff.at[:, n]) if n < NZ else (FIRST, REST, yhg, yfg)
@@ -342,18 +382,23 @@
         def _():
             wait(block, vzs.at[z0])
 
+        wait(ab.at[edge, z0, amp_half(0)], ayf.at[z0])
+
         @pl.when(active)
         def _():
-            for k in range(NY - 1):
+            for k in range(2):
                 wait(ab.at[edge, z0], ays.at[k, z0])
 
-            @pl.when(n > 0)
-            def _():
-                wait(ab.at[edge, z0], azs.at[z0])
-
         return carry
 
     lax.fori_loop(0, NZ, sent, 0)
+
+    @pl.when(active)
+    def _():
+        wait(ab.at[edge, z], azs.at[NZ])
+        for d in (0, 1, -1, 2, -2, 3):
+            wait(ab.at[edge, z], azs.at[mod(z - d, NZ)])
+
     for n in range(NZ + 1):
         lo, size, hb, fb_ = span(n)
 
@@ -378,8 +423,6 @@
 
 def body(amplitudes, vectors, pair_count, tile_map):
     live = lax.broadcasted_iota(jnp.int32, (BLOCKS, 1, SLOTS), 2) < pair_count[:, None, None]
-    amp = jnp.where(live, amplitudes, jnp.zeros_like(amplitudes))
-    near = jnp.sum(tile_map[:, :, None] == jnp.arange(TOTAL)[None, None, :], axis=1).astype(jnp.bfloat16)
     f32, bf16 = jnp.float32, jnp.bfloat16
     dma = pltpu.SemaphoreType.DMA
     out = pl.pallas_call(
@@ -388,13 +431,17 @@
         in_specs=[
             pl.BlockSpec(memory_space=pltpu.VMEM),
             pl.BlockSpec(memory_space=pl.ANY),
+            pl.BlockSpec(memory_space=pltpu.SMEM),
             pl.BlockSpec(memory_space=pltpu.VMEM),
         ],
         out_specs=pl.BlockSpec(memory_space=pltpu.VMEM),
         scratch_shapes=[
+            pltpu.VMEM(amplitudes.shape, bf16),
+            pltpu.VMEM((TOTAL, 2 * TOTAL), bf16),
             pltpu.VMEM((NZ, GROUP, DEPTH, SLOTS), bf16),
             pltpu.VMEM((2, NZ, GROUP, ROWS, SLOTS), bf16),
-            pltpu.VMEM((2, 2 * ROWS * PITCH, SLOTS), f32),
+            pltpu.VMEM((2 * ROWS * PITCH, SLOTS), f32),
+            pltpu.VMEM((8 * PITCH, SLOTS), f32),
             pltpu.VMEM((2, NZ, GROUP, ROWS, SLOTS), f32),
             pltpu.VMEM((2, 4, 2, REST, ROWS, SLOTS), f32),
             pltpu.VMEM((2, 4, FIRST, ROWS, SLOTS), f32),
@@ -408,8 +455,8 @@
             dma((4, NZ)), dma((4, NZ)),
             dma((4, NZ)), dma((4, NZ)),
             dma((NX,)), dma((NX, NC)),
-            dma((NZ,)), dma((NZ,)),
-            dma((NY - 1, NZ)), dma((2, NZ)),
+            dma((NZ + 1,)), dma((NZ,)),
+            dma((2, NZ)), dma((NZ,)), dma((3, NZ)),
             dma((2, 4)), dma((2, 4)),
             dma((2, 4)), dma((2, 4)),
             dma((2, NZ + 1)), dma((NZ + 1,)),
@@ -420,7 +467,7 @@
             collective_id=0, has_side_effects=True, vmem_limit_bytes=60 * 2**20
         ),
         cost_estimate=pl.CostEstimate(flops=12 * 10**9, bytes_accessed=4 * 10**6, transcendentals=0),
-    )(amp, vectors, near)
+    )(amplitudes, vectors, pair_count, tile_map)
     return jnp.where(live, out, jnp.zeros_like(out))
 
 

time: 141 us -> 134 us (0.950)
  other arithmetic: 10 us -> 1.55 us
    reduce_sum x1 -> x0, other arithmetic: 5.69 us -> none  [body(): jnp.sum(tile_map[:, :, None] == jnp.arange(TOTAL)[None, None, :], axis=1)]
    select_n x1 -> x0, other arithmetic: 1.48 us -> none  [body(): amp = jnp.where(live, amplitudes, jnp.zeros_like(amplitudes))]
where the time goes in v3:
time: 134 us
  Pallas kernels  130 us (97%)
  other arithmetic  1.55 us (1%)
  local copies, waits for them, and re-layouts  1.51 us (1%)
    pallas_call x1, Pallas kernels, body(): pl.pallas_call(kernel, out_shape=jax.ShapeDtypeStruct(amplitudes.shape, b...  130 us

profile of v3, /device:TPU:1, one launch (start us, length us, event | category | flops | bytes accessed | tf_op | source)
XLA Modules:
  0.0 133.6 jit_solution(3651897463117721339)
XLA Ops:
  0.0 1.5 %copy.5.tiles = s32[256,32]{1,0:T(8,128)} copy(s32[256,32]{0,1:T(8,128)} %param.7) | data formatting | bytes 65536 | tf_op args[3]
  1.5 0.0 copy-start
  1.5 130.5 %shard_map.46 = bf16[4,64,128]{2,1,0:T(8,128)(2,1)} custom-call(bf16[4,64,128]{2,1,0:T(8,128)(2,1)} %amp_in.1, bf16[4,1280,128]{2,1,0:T(8,128)(2,1)} %vec.1, s32[4]{0:T(128)} %counts.1, s32[256,32]{1,0:T(8,128)} %copy.5.tiles), custom_call_target="tpu_custom_call" | custom-call | flops 12000000000 | bytes 4000000 | tf_op jit(solution)/shard_map/pallas_call | solution.py:428
  132.0 0.0 copy-done
  132.0 0.1 iota_compare_fusion
  132.1 1.5 %broadcast_select_fusion = bf16[4,64,128]{2,1,0:T(8,128)(2,1)} fusion(bf16[4,64,128]{2,1,0:T(8,128)(2,1)} %shard_map.46, pred[4,128]{1,0:T(4,128)(4,1)S(1)} %iota_compare_fusion), kind=kLoop, calls=%fused_computation | loop fusion | flops 32768 | bytes 131584 | tf_op jit(solution)/shard_map/jit(_where)/select_n | solution.py:471
Async XLA Ops:
  1.5 130.5 %copy-start = (s32[4]{0:T(128)S(1)}, s32[4]{0:T(128)}, u32[]{:S(2)}) copy-start(s32[4]{0:T(128)} %counts.1) | copy-start | bytes 52

commit v4 on v3

--- a/solution.py
+++ b/solution.py
@@ -14,6 +14,7 @@
 ROWS = 16
 PITCH = TOTAL + 8
 FOLD = SLOTS // (DEPTH - SLOTS)
+AHEAD = 3
 FIRST = 20
 REST = GROUP - FIRST
 
@@ -96,12 +97,18 @@
             def _():
                 send(src, dst, axs.at[0], axr.at[x, c], c1=home)
 
-    for d in (1, -1, 2, -2, 3, -3, 4):
-        z1 = mod(z + d, NZ)
+    def away_from(s):
+        return jnp.where(lax.rem(s, 2) == 1, lax.div(s + 1, 2), -lax.div(s, 2))
+
+    def hand_out(s):
+        z1 = mod(z + away_from(s), NZ)
         send(vec.at[:, rows(z1), :], vb.at[z, mine(x, c)], vzs.at[z1], vzr.at[z], z1=z1)
 
+    for s in range(1, AHEAD):
+        hand_out(jnp.int32(s))
+
     def source(s):
-        return mod(z - jnp.where(lax.rem(s, 2) == 1, lax.div(s + 1, 2), -lax.div(s, 2)), NZ)
+        return mod(z - away_from(s), NZ)
 
     around = mod(y - 2 * c, NY)
     near_e, other_e = 1 - lax.rem(around, 2), lax.rem(around, 2)
@@ -154,6 +161,11 @@
             z0 = source(s)
             block = vb.at[z0, mine(x, c)]
             wait(block, vzr.at[z0])
+
+            @pl.when(s < NZ - AHEAD)
+            def _():
+                hand_out(s + AHEAD)
+
             send(block, block, xs.at[0, z0], xr.at[0, z0], x1=xp)
             send(block, block, xs.at[1, z0], xr.at[1, z0], x1=xm)
             send(block, block, ss.at[0, z0], sr.at[0, z0], c1=mate)

time: 134 us -> 121 us (0.903)
  Pallas kernels: 130 us -> 118 us
    pallas_call x1, Pallas kernels: 130 us -> 118 us  [body(): pl.pallas_call(kernel, out_shape=jax.ShapeDtypeStruct(amplitudes.shape, b...]
where the time goes in v4:
time: 121 us
  Pallas kernels  118 us (98%)
  other arithmetic  1.55 us (1%)
  local copies, waits for them, and re-layouts  1.51 us (1%)
    pallas_call x1, Pallas kernels, body(): pl.pallas_call(kernel, out_shape=jax.ShapeDtypeStruct(amplitudes.shape, b...  118 us

profile of v4, /device:TPU:1, one launch (start us, length us, event | category | flops | bytes accessed | tf_op | source)
XLA Modules:
  0.0 120.8 jit_solution(17224649670331355374)
XLA Ops:
  0.0 1.5 %copy.5.tiles = s32[256,32]{1,0:T(8,128)} copy(s32[256,32]{0,1:T(8,128)} %param.7) | data formatting | bytes 65536 | tf_op args[3]
  1.5 0.0 copy-start
  1.5 117.8 %shard_map.46 = bf16[4,64,128]{2,1,0:T(8,128)(2,1)} custom-call(bf16[4,64,128]{2,1,0:T(8,128)(2,1)} %amp_in.1, bf16[4,1280,128]{2,1,0:T(8,128)(2,1)} %vec.1, s32[4]{0:T(128)} %counts.1, s32[256,32]{1,0:T(8,128)} %copy.5.tiles), custom_call_target="tpu_custom_call" | custom-call | flops 12000000000 | bytes 4000000 | tf_op jit(solution)/shard_map/pallas_call | solution.py:440
  119.3 0.0 copy-done
  119.3 0.1 iota_compare_fusion
  119.4 1.5 %broadcast_select_fusion = bf16[4,64,128]{2,1,0:T(8,128)(2,1)} fusion(bf16[4,64,128]{2,1,0:T(8,128)(2,1)} %shard_map.46, pred[4,128]{1,0:T(4,128)(4,1)S(1)} %iota_compare_fusion), kind=kLoop, calls=%fused_computation | loop fusion | flops 32768 | bytes 131584 | tf_op jit(solution)/shard_map/jit(_where)/select_n | solution.py:483
Async XLA Ops:
  1.5 117.8 %copy-start = (s32[4]{0:T(128)S(1)}, s32[4]{0:T(128)}, u32[]{:S(2)}) copy-start(s32[4]{0:T(128)} %counts.1) | copy-start | bytes 52

commit v5 on v3

--- a/solution.py
+++ b/solution.py
@@ -14,6 +14,7 @@
 ROWS = 16
 PITCH = TOTAL + 8
 FOLD = SLOTS // (DEPTH - SLOTS)
+AHEAD = 3
 FIRST = 20
 REST = GROUP - FIRST
 
@@ -29,7 +30,7 @@
 
 def kernel(
     amp_in, vec, counts, tiles, out,
-    amp, near, vb, ab, w, wt, o, gzb, fzb, yhf, yff, yhg, yfg, fb, fr,
+    amp, near, vb, ab, w, wt, u, ut, o, gzb, fzb, yhf, yff, yhg, yfg, fb, fr,
     vzs, vzr, xs, xr, ss, sr, axs, axr, azs, azr, ays, ayf, ayr,
     gzs, gzr, fzs, fzr, yhs, yhr, yfs, yfr, es, er,
 ):
@@ -43,6 +44,12 @@
             src_ref=src, dst_ref=dst, send_sem=ssem, recv_sem=rsem,
             device_id=(z1, x1, c1, y1), device_id_type=pl.DeviceIdType.MESH,
         ).start()
+
+    def away_from(s):
+        return jnp.where(lax.rem(s, 2) == 1, lax.div(s + 1, 2), -lax.div(s, 2))
+
+    def source(s):
+        return mod(z - away_from(s), NZ)
 
     zp, zm = mod(z + 1, NZ), mod(z - 1, NZ)
     xp, xm, xo = mod(x + 1, NX), mod(x - 1, NX), mod(x + 2, NX)
@@ -78,6 +85,22 @@
         greet(y1=mod(y + d, NY))
     for b in range(BLOCKS):
         amp[b] = jnp.where(slot < counts[b], amp_in[b], jnp.zeros_like(amp_in[b]))
+
+    column = lax.broadcasted_iota(jnp.int32, (32, TOTAL), 1)
+    block_of = source(lax.div(column, GROUP)) * GROUP + lax.rem(column, GROUP)
+
+    def adjacency(n, carry):
+        at = pl.ds(pl.multiple_of(n * 32, 32), 32)
+        named = tiles[at, :]
+        found = jnp.zeros((32, TOTAL), jnp.float32)
+        for j in range(tiles.shape[1]):
+            found = found + jnp.where(named[:, j : j + 1] == block_of, 1.0, 0.0)
+        found = found.astype(jnp.bfloat16)
+        for k in range(4):
+            near[at, k * SLOTS : (k + 1) * SLOTS] = found[:, k // 2 * SLOTS : (k // 2 + 1) * SLOTS]
+        return carry
+
+    lax.fori_loop(0, TOTAL // 32, adjacency, 0)
     pl.semaphore_wait(barrier, NZ - 1 + NX * NC - 1 + NY - 1)
 
     for d in range(NX):
@@ -96,12 +119,9 @@
             def _():
                 send(src, dst, axs.at[0], axr.at[x, c], c1=home)
 
-    for d in (1, -1, 2, -2, 3, -3, 4):
-        z1 = mod(z + d, NZ)
+    def hand_out(s):
+        z1 = mod(z + away_from(s), NZ)
         send(vec.at[:, rows(z1), :], vb.at[z, mine(x, c)], vzs.at[z1], vzr.at[z], z1=z1)
-
-    def source(s):
-        return mod(z - jnp.where(lax.rem(s, 2) == 1, lax.div(s + 1, 2), -lax.div(s, 2)), NZ)
 
     around = mod(y - 2 * c, NY)
     near_e, other_e = 1 - lax.rem(around, 2), lax.rem(around, 2)
@@ -117,46 +137,81 @@
         send(block, block, ays.at[0, z0], ayr.at[0, z0], y1=yp)
         send(block, block, ays.at[1, z0], ayr.at[0, z0], y1=ym)
 
-    def products(z0):
-        @pl.when(jnp.logical_not(active))
-        def _():
+    def products(s, z0, x0, c0):
+        for b in range(BLOCKS):
+            q = x0 * (NC * BLOCKS) + c0 * BLOCKS + b
+            a = jnp.concatenate([ab[0, z0, q], ab[1, z0, q]], axis=0)
+            r = lax.dot_general(a, vb[z0, q], (((1,), (1,)), ((), ())), preferred_element_type=jnp.float32)
+            w[pl.ds(s * GROUP + q, 2 * ROWS, stride=PITCH), :] = r[:, :SLOTS]
+            tail = [r[m * 8 : m * 8 + 8, SLOTS:] for m in range(FOLD)]
+            wt[pl.ds(s * GROUP + q, 8, stride=PITCH), :] = jnp.concatenate(tail, axis=1)
+
+    def mix(src, dst, half):
+        def some(i, carry):
+            at = [pl.multiple_of((2 * i + h) * PITCH, 8) for h in range(2)]
+            hi, lo = split(jnp.concatenate([src[pl.ds(a + half * SLOTS, SLOTS), :] for a in at], axis=1))
+            pairs = near[:, half * TOTAL : (half + 1) * TOTAL]
+            r = jnp.dot(pairs, jnp.concatenate([hi, lo], axis=0), preferred_element_type=jnp.float32)
             for h in range(2):
-                wait(ab.at[other_e, z0, amp_half(h)], ayr.at[1 + h, z0])
-
-        def some(n, carry):
-            for u in range(4):
-                q = n * 4 + u
-                a = jnp.concatenate([ab[0, z0, q], ab[1, z0, q]], axis=0)
-                r = lax.dot_general(a, vb[z0, q], (((1,), (1,)), ((), ())), preferred_element_type=jnp.float32)
-                w[pl.ds(z0 * GROUP + q, 2 * ROWS, stride=PITCH), :] = r[:, :SLOTS]
-                tail = [r[m * 8 : m * 8 + 8, SLOTS:] for m in range(FOLD)]
-                wt[pl.ds(z0 * GROUP + q, 8, stride=PITCH), :] = jnp.concatenate(tail, axis=1)
+                to = pl.ds(at[h], TOTAL)
+                part_sum = r[:, h * SLOTS : (h + 1) * SLOTS]
+                dst[to, :] = dst[to, :] + part_sum if half else part_sum
             return carry
 
-        lax.fori_loop(0, GROUP // 4, some, 0)
-
-    def adjacency(n, carry):
-        at = pl.ds(pl.multiple_of(n * 32, 32), 32)
-        named = tiles[at, :]
-        block = lax.broadcasted_iota(jnp.int32, (32, TOTAL), 1)
-        found = jnp.zeros((32, TOTAL), jnp.float32)
-        for j in range(tiles.shape[1]):
-            found = found + jnp.where(named[:, j : j + 1] == block, 1.0, 0.0)
-        near[at, :TOTAL] = found.astype(jnp.bfloat16)
-        near[at, TOTAL:] = found.astype(jnp.bfloat16)
-        return carry
-
-    lax.fori_loop(0, TOTAL // 32, adjacency, 0)
+        lax.fori_loop(0, src.shape[0] // PITCH // 2, some, 0)
+
+    def spread(z0):
+        block = vb.at[z0, mine(x, c)]
+        send(block, block, xs.at[0, z0], xr.at[0, z0], x1=xp)
+        send(block, block, xs.at[1, z0], xr.at[1, z0], x1=xm)
+        send(block, block, ss.at[0, z0], sr.at[0, z0], c1=mate)
+
+    wait(vb.at[z, mine(x, c)], vzr.at[z])
+    spread(z)
+
+    @pl.when(active)
+    def _():
+        for x0 in range(NX):
+            for c0 in range(NC):
+                wait(ab.at[edge, z, mine(x0, c0)], axr.at[x0, c0])
+        block = ab.at[edge, z]
+        send(block, block, azs.at[z], azr.at[z], z1=zp)
+        send(block, block, azs.at[NZ], azr.at[z], z1=zm)
+        spread_amp(z)
+
+    for s in range(1, AHEAD + 1):
+        hand_out(jnp.int32(s))
 
     def step(s, carry):
-        @pl.when(s < NZ)
+        @pl.when(jnp.logical_and(jnp.logical_and(s >= 1, s < NZ), active))
         def _():
             z0 = source(s)
-            block = vb.at[z0, mine(x, c)]
-            wait(block, vzr.at[z0])
-            send(block, block, xs.at[0, z0], xr.at[0, z0], x1=xp)
-            send(block, block, xs.at[1, z0], xr.at[1, z0], x1=xm)
-            send(block, block, ss.at[0, z0], sr.at[0, z0], c1=mate)
+            block = ab.at[edge, z0]
+            wait(block, azr.at[z0])
+
+            @pl.when(s < NZ - 2)
+            def _():
+                send(block, block, azs.at[z0], azr.at[z0], z1=jnp.where(lax.rem(s, 2) == 1, zp, zm))
+
+            spread_amp(z0)
+
+        @pl.when(jnp.logical_and(s >= 1, s < NZ + 1))
+        def _():
+            z0 = source(s - 1)
+            wait(ab.at[near_e, z0], ayr.at[0, z0])
+            half = ab.at[near_e, z0, amp_half(side)]
+            send(half, half, ayf.at[z0], ayr.at[1 + side, z0], y1=away)
+
+        @pl.when(jnp.logical_and(s >= 1, s < NZ))
+        def _():
+            z0 = source(s)
+            wait(vb.at[z0, mine(x, c)], vzr.at[z0])
+
+            @pl.when(s < NZ - AHEAD)
+            def _():
+                hand_out(s + AHEAD)
+
+            spread(z0)
 
         @pl.when(jnp.logical_and(s >= 1, s < NZ + 1))
         def _():
@@ -171,77 +226,55 @@
             send(half, half, xs.at[3, z0], xr.at[3, z0], x1=xm)
             send(right, right, ss.at[2, z0], sr.at[2, z0], c1=mate)
 
-        @pl.when(jnp.logical_and(s == 0, active))
-        def _():
-            for x0 in range(NX):
-                for c0 in range(NC):
-                    wait(ab.at[edge, z, mine(x0, c0)], axr.at[x0, c0])
-            block = ab.at[edge, z]
-            send(block, block, azs.at[z], azr.at[z], z1=zp)
-            send(block, block, azs.at[NZ], azr.at[z], z1=zm)
-            spread_amp(z)
-
-        @pl.when(jnp.logical_and(jnp.logical_and(s >= 1, s < NZ), active))
-        def _():
-            z0 = source(s)
-            block = ab.at[edge, z0]
-            wait(block, azr.at[z0])
-
-            @pl.when(s < NZ - 2)
+        @pl.when(jnp.logical_and(s >= 2, s < NZ + 2))
+        def _():
+            z0 = source(s - 2)
+
+            @pl.when(jnp.logical_not(active))
             def _():
-                send(block, block, azs.at[z0], azr.at[z0], z1=jnp.where(lax.rem(s, 2) == 1, zp, zm))
-
-            spread_amp(z0)
-
-        @pl.when(jnp.logical_and(s >= 1, s < NZ + 1))
-        def _():
-            z0 = source(s - 1)
-            wait(ab.at[near_e, z0], ayr.at[0, z0])
-            half = ab.at[near_e, z0, amp_half(side)]
-            send(half, half, ayf.at[z0], ayr.at[1 + side, z0], y1=away)
-
-        @pl.when(jnp.logical_and(s >= 2, s < NZ + 2))
-        def _():
-            z0 = source(s - 2)
+                for h in range(2):
+                    wait(ab.at[other_e, z0, amp_half(h)], ayr.at[1 + h, z0])
+
+            for x0 in (x, xm, xp):
+                products(s - 2, z0, x0, c)
+            wait(vb.at[z0, mine(x, mate)], sr.at[0, z0])
+            products(s - 2, z0, x, mate)
             wait(vb.at[z0, part(xo, c, 0)], xr.at[2, z0])
             wait(vb.at[z0, part(xo, c, 1)], xr.at[3, z0])
             block = vb.at[z0, mine(xo, c)]
             send(block, block, ss.at[3, z0], sr.at[3, z0], c1=mate)
+            products(s - 2, z0, xo, c)
+            for k, x0 in ((1, xm), (2, xp)):
+                wait(vb.at[z0, mine(x0, mate)], sr.at[k, z0])
+                products(s - 2, z0, x0, mate)
 
         @pl.when(s >= 3)
         def _():
             z0 = source(s - 3)
-            for k, x0 in enumerate((x, xm, xp, xo)):
-                wait(vb.at[z0, mine(x0, mate)], sr.at[k, z0])
-            products(z0)
+            wait(vb.at[z0, mine(xo, mate)], sr.at[3, z0])
+            products(s - 3, z0, xo, mate)
+
+        @pl.when(s == NZ - 1)
+        def _():
+            mix(w, u, 0)
+            mix(wt, ut, 0)
 
         return carry
 
     lax.fori_loop(0, NZ + 3, step, 0)
 
-    def mix(ref):
-        def some(i, carry):
-            at = [pl.ds(pl.multiple_of((2 * i + h) * PITCH, 8), TOTAL) for h in range(2)]
-            hi, lo = split(jnp.concatenate([ref[a, :] for a in at], axis=1))
-            u = jnp.dot(near[...], jnp.concatenate([hi, lo], axis=0), preferred_element_type=jnp.float32)
-            for h in range(2):
-                ref[at[h], :] = u[:, h * SLOTS : (h + 1) * SLOTS]
-            return carry
-
-        lax.fori_loop(0, ref.shape[0] // PITCH // 2, some, 0)
-
-    mix(w)
-    mix(wt)
+    mix(w, u, 1)
+    mix(wt, ut, 1)
     row = lax.broadcasted_iota(jnp.int32, (2 * ROWS, SLOTS), 0)
     lane = lax.broadcasted_iota(jnp.int32, (2 * ROWS, SLOTS), 1)
     own_fold = lax.div(row, 8) == lax.div(lane, DEPTH - SLOTS)
 
     def residuals(zt):
         def some(n, carry):
-            for u in range(4):
-                p = n * 4 + u
-                full = w[pl.ds(zt * GROUP + p, 2 * ROWS, stride=PITCH), :]
-                tail = jnp.concatenate([wt[pl.ds(zt * GROUP + p, 8, stride=PITCH), :]] * FOLD, axis=0)
+            for step_in in range(4):
+                p = n * 4 + step_in
+                full = u[pl.ds(zt * GROUP + p, 2 * ROWS, stride=PITCH), :]
+                tail = jnp.concatenate([ut[pl.ds(zt * GROUP + p, 8, stride=PITCH), :]] * FOLD, axis=0)
                 u2 = jnp.concatenate([full, jnp.where(own_fold, tail, 0.0)], axis=1)
                 left = jnp.concatenate(split(u2), axis=0)
                 right = jnp.concatenate([vb[zt, p, :SLOTS, :]] + [vb[zt, p, SLOTS:, :]] * FOLD, axis=0)
@@ -281,14 +314,20 @@
             at = pl.ds(lo, size)
             o[other_e, zt, at] = o[other_e, zt, at] + (fb_[0] + fb_[1])
 
-    def gview(zt, t, k):
-        return o.at[pl.ds(k, 1), zt, pl.ds(FIRST, REST)] if t == 0 else o.at[:, zt, pl.ds(FIRST, REST)]
+    def gview(e):
+        def view(zt, t, k):
+            return o.at[e, zt, pl.ds(FIRST + k * (REST // 2), REST // 2)] if t == 0 else o.at[e, zt, pl.ds(FIRST, REST)]
+
+        return view
 
     def fview(zt, t, k):
         return o.at[other_e, zt, pl.ds(k * (FIRST // 2), FIRST // 2)] if t == 0 else o.at[other_e, zt, pl.ds(0, FIRST)]
 
-    def gland(t, k):
-        return gzb.at[k, t, pl.ds(0, 1)] if t == 0 else gzb.at[k, t]
+    def gland(e):
+        def land(t, k):
+            return gzb.at[e, k, t, pl.ds(0, REST // 2)] if t == 0 else gzb.at[e, k, t]
+
+        return land
 
     def fland(t, k):
         return fzb.at[k, t, pl.ds(0, FIRST // 2)] if t == 0 else fzb.at[k, t]
@@ -316,12 +355,48 @@
                 zrecv(view, land, rsem, k, 3)
 
     def g(m):
-        zwork(m, gview, gland, gzs, gzr)
+        for e in range(2):
+            zwork(m, gview(e), gland(e), gzs.at[e], gzr.at[e])
 
     def f(m):
         @pl.when(active)
         def _():
             zwork(m, fview, fland, fzs, fzr)
+
+    def sent(n):
+        z0 = mod(z + n, NZ)
+        block, half = vb.at[z0, mine(x, c)], vb.at[z0, part(x, c, 0)]
+        for k in range(2):
+            wait(block, xs.at[k, z0])
+            wait(half, xs.at[2 + k, z0])
+        for k in range(4):
+            wait(block, ss.at[k, z0])
+
+        if n > 0:
+            wait(block, vzs.at[z0])
+
+        wait(ab.at[edge, z0, amp_half(0)], ayf.at[z0])
+
+        @pl.when(active)
+        def _():
+            for k in range(2):
+                wait(ab.at[edge, z0], ays.at[k, z0])
+
+    def sent_first():
+        piece = amp.at[:, pl.ds(0, ROWS), :]
+        for d in range(1, NX):
+            wait(piece, axs.at[d])
+
+        @pl.when(c != home)
+        def _():
+            wait(piece, axs.at[0])
+
+
+        @pl.when(active)
+        def _():
+            wait(ab.at[edge, z], azs.at[NZ])
+            for d in (0, 1, -1, 2, -2, 3):
+                wait(ab.at[edge, z], azs.at[mod(z - d, NZ)])
 
     order = [mod(z + d, NZ) for d in (4, 3, -3, 2, -2, 1, -1, 0)]
     for n in range(NZ):
@@ -334,6 +409,8 @@
         if n >= 2:
             y3(n - 2, order[n - 2])
             f(n - 2)
+        sent(n)
+    sent_first()
     y2(7, z)
     y3(6, order[6])
     f(6)
@@ -357,48 +434,6 @@
                 else:
                     pltpu.make_async_copy(src, dst, er.at[x]).start()
 
-    for x0 in range(NX):
-        wait(fr.at[:, pl.ds(x0 * ROWS, ROWS), :], er.at[x0])
-    out[...] = fr[...]
-
-    piece = amp.at[:, pl.ds(0, ROWS), :]
-    for d in range(1, NX):
-        wait(piece, axs.at[d])
-
-    @pl.when(c != home)
-    def _():
-        wait(piece, axs.at[0])
-
-    def sent(n, carry):
-        z0 = mod(z + n, NZ)
-        block, half = vb.at[z0, mine(x, c)], vb.at[z0, part(x, c, 0)]
-        for k in range(2):
-            wait(block, xs.at[k, z0])
-            wait(half, xs.at[2 + k, z0])
-        for k in range(4):
-            wait(block, ss.at[k, z0])
-
-        @pl.when(n > 0)
-        def _():
-            wait(block, vzs.at[z0])
-
-        wait(ab.at[edge, z0, amp_half(0)], ayf.at[z0])
-
-        @pl.when(active)
-        def _():
-            for k in range(2):
-                wait(ab.at[edge, z0], ays.at[k, z0])
-
-        return carry
-
-    lax.fori_loop(0, NZ, sent, 0)
-
-    @pl.when(active)
-    def _():
-        wait(ab.at[edge, z], azs.at[NZ])
-        for d in (0, 1, -1, 2, -2, 3):
-            wait(ab.at[edge, z], azs.at[mod(z - d, NZ)])
-
     for n in range(NZ + 1):
         lo, size, hb, fb_ = span(n)
 
@@ -410,7 +445,8 @@
         wait(fb_.at[0], yfs.at[n])
     for k in range(2):
         for t in range(4):
-            wait(gland(t, k), gzs.at[k, t])
+            for e in range(2):
+                wait(gland(e)(t, k), gzs.at[e, k, t])
 
     @pl.when(active)
     def _():
@@ -419,6 +455,10 @@
                 wait(fland(t, k), fzs.at[k, t])
         for n in range(1, NX * NC):
             wait(fb.at[pl.ds(0, BLOCKS)], es.at[n])
+
+    for x0 in range(NX):
+        wait(fr.at[:, pl.ds(x0 * ROWS, ROWS), :], er.at[x0])
+    out[...] = fr[...]
 
 
 def body(amplitudes, vectors, pair_count, tile_map):
@@ -442,8 +482,10 @@
             pltpu.VMEM((2, NZ, GROUP, ROWS, SLOTS), bf16),
             pltpu.VMEM((2 * ROWS * PITCH, SLOTS), f32),
             pltpu.VMEM((8 * PITCH, SLOTS), f32),
+            pltpu.VMEM((2 * ROWS * PITCH, SLOTS), f32),
+            pltpu.VMEM((8 * PITCH, SLOTS), f32),
             pltpu.VMEM((2, NZ, GROUP, ROWS, SLOTS), f32),
-            pltpu.VMEM((2, 4, 2, REST, ROWS, SLOTS), f32),
+            pltpu.VMEM((2, 2, 4, REST, ROWS, SLOTS), f32),
             pltpu.VMEM((2, 4, FIRST, ROWS, SLOTS), f32),
             pltpu.VMEM((NZ, FIRST // 2, ROWS, SLOTS), f32),
             pltpu.VMEM((2, NZ, FIRST, ROWS, SLOTS), f32),
@@ -457,7 +499,7 @@
             dma((NX,)), dma((NX, NC)),
             dma((NZ + 1,)), dma((NZ,)),
             dma((2, NZ)), dma((NZ,)), dma((3, NZ)),
-            dma((2, 4)), dma((2, 4)),
+            dma((2, 2, 4)), dma((2, 2, 4)),
             dma((2, 4)), dma((2, 4)),
             dma((2, NZ + 1)), dma((NZ + 1,)),
             dma((NZ + 1,)), dma((2, NZ + 1)),

time: 134 us -> 116 us (0.87)
  Pallas kernels: 130 us -> 113 us
    pallas_call x1, Pallas kernels: 130 us -> 113 us  [body(): pl.pallas_call(kernel, out_shape=jax.ShapeDtypeStruct(amplitudes.shape, b...]
where the time goes in v5:
time: 116 us
  Pallas kernels  113 us (97%)
  other arithmetic  1.55 us (1%)
  local copies, waits for them, and re-layouts  1.51 us (1%)
    pallas_call x1, Pallas kernels, body(): pl.pallas_call(kernel, out_shape=jax.ShapeDtypeStruct(amplitudes.shape, b...  113 us

profile of v5, /device:TPU:1, one launch (start us, length us, event | category | flops | bytes accessed | tf_op | source)
XLA Modules:
  0.0 116.0 jit_solution(18396822645059057785)
XLA Ops:
  0.0 1.5 %copy.5.tiles = s32[256,32]{1,0:T(8,128)} copy(s32[256,32]{0,1:T(8,128)} %param.7) | data formatting | bytes 65536 | tf_op args[3]
  1.5 0.0 copy-start
  1.5 112.9 %shard_map.46 = bf16[4,64,128]{2,1,0:T(8,128)(2,1)} custom-call(bf16[4,64,128]{2,1,0:T(8,128)(2,1)} %amp_in.1, bf16[4,1280,128]{2,1,0:T(8,128)(2,1)} %vec.1, s32[4]{0:T(128)} %counts.1, s32[256,32]{1,0:T(8,128)} %copy.5.tiles), custom_call_target="tpu_custom_call" | custom-call | flops 12000000000 | bytes 4000000 | tf_op jit(solution)/shard_map/pallas_call | solution.py:468
  114.5 0.0 copy-done
  114.5 0.1 iota_compare_fusion
  114.5 1.5 %broadcast_select_fusion = bf16[4,64,128]{2,1,0:T(8,128)(2,1)} fusion(bf16[4,64,128]{2,1,0:T(8,128)(2,1)} %shard_map.46, pred[4,128]{1,0:T(4,128)(4,1)S(1)} %iota_compare_fusion), kind=kLoop, calls=%fused_computation | loop fusion | flops 32768 | bytes 131584 | tf_op jit(solution)/shard_map/jit(_where)/select_n | solution.py:513
Async XLA Ops:
  1.5 113.0 %copy-start = (s32[4]{0:T(128)S(1)}, s32[4]{0:T(128)}, u32[]{:S(2)}) copy-start(s32[4]{0:T(128)} %counts.1) | copy-start | bytes 52

commit v6 on v5

--- a/solution.py
+++ b/solution.py
@@ -17,6 +17,22 @@
 AHEAD = 3
 FIRST = 20
 REST = GROUP - FIRST
+G_HOPS = ((4, 2), (3, 2), (2, 1), (1, 0))
+F_HOPS = ((4, 2), (3, 2), (2, 0), (1, 0))
+F_LAST = tuple(i for i, (_, d) in enumerate(F_HOPS) if d == 0)
+ORDER = (
+    ("R", 0), ("g", 0, 0, 0), ("g", 0, 1, 0), ("g", 1, 0, 0), ("g", 1, 1, 0), ("y1", 0),
+    ("R", 1), ("g", 0, 0, 1), ("g", 1, 0, 1), ("y1", 1), ("R", 2), ("g", 0, 1, 1),
+    ("g", 1, 1, 1), ("y1", 2), ("R", 3), ("y2", 0), ("y1", 3), ("R", 4),
+    ("y2", 1), ("y1", 4), ("R", 5), ("g", 0, 0, 2), ("g", 0, 1, 2), ("y2", 2),
+    ("y1", 5), ("R", 6), ("g", 1, 0, 2), ("g", 1, 1, 2), ("y3", 0), ("f", 0, 0),
+    ("f", 1, 0), ("y2", 3), ("y1", 6), ("R", 7), ("y3", 1), ("f", 0, 1),
+    ("g", 0, 0, 3), ("g", 0, 1, 3), ("y2", 4), ("y1", 7), ("y3", 2), ("f", 1, 1),
+    ("y2", 5), ("g", 1, 0, 3), ("g", 1, 1, 3), ("y3", 3), ("y2", 6), ("f", 0, 2),
+    ("gr", 0, 1), ("y3", 4), ("y2", 7), ("gr", 0, 0), ("f", 1, 2), ("y3", 5),
+    ("f", 0, 3), ("gr", 1, 0), ("gr", 1, 1), ("gfin",), ("y3", 6), ("f", 1, 3),
+    ("y3", 7), ("fown",),
+)
 
 
 def split(x):
@@ -30,9 +46,9 @@
 
 def kernel(
     amp_in, vec, counts, tiles, out,
-    amp, near, vb, ab, w, wt, u, ut, o, gzb, fzb, yhf, yff, yhg, yfg, fb, fr,
+    amp, near, vb, ab, w, wt, u, ut, o, gzb, fzb, yhf, yff, fin,
     vzs, vzr, xs, xr, ss, sr, axs, axr, azs, azr, ays, ayf, ayr,
-    gzs, gzr, fzs, fzr, yhs, yhr, yfs, yfr, es, er,
+    gzs, gzr, fzs, fzr, yhs, yhr, yfs, yfr, ffs, fos, fns, finr,
 ):
     z, x, c, y = (lax.axis_index(a) for a in ("z", "x", "c", "y"))
 
@@ -286,82 +302,105 @@
 
         lax.fori_loop(0, GROUP // 4, some, 0)
 
-    def span(n):
-        return (0, FIRST, yhf.at[n], yff.at[:, n]) if n < NZ else (FIRST, REST, yhg, yfg)
-
     def y1(n, zt):
-        lo, size, hb, _ = span(n)
-
         @pl.when(jnp.logical_not(active))
         def _():
-            send(o.at[other_e, zt, pl.ds(lo, size // 2)], hb, yhs.at[0, n], yhr.at[n], y1=ym)
-            send(o.at[other_e, zt, pl.ds(lo + size // 2, size // 2)], hb, yhs.at[1, n], yhr.at[n], y1=yp)
+            for h, y1_ in enumerate((ym, yp)):
+                half = o.at[other_e, zt, pl.ds(h * (FIRST // 2), FIRST // 2)]
+                send(half, yhf.at[n], yhs.at[h, n], yhr.at[n], y1=y1_)
 
     def y2(n, zt):
-        lo, size, hb, fb_ = span(n)
-        wait(hb, yhr.at[n])
-        at = pl.ds(lo + side * (size // 2), size // 2)
-        o[near_e, zt, at] = o[near_e, zt, at] + hb[...]
-        send(o.at[near_e, zt, pl.ds(lo, size)], fb_.at[side], yfs.at[n], yfr.at[side, n], y1=onward)
+        wait(yhf.at[n], yhr.at[n])
+        at = pl.ds(side * (FIRST // 2), FIRST // 2)
+        o[near_e, zt, at] = o[near_e, zt, at] + yhf[n]
+        send(o.at[near_e, zt, pl.ds(0, FIRST)], yff.at[side, n], yfs.at[n], yfr.at[side, n], y1=onward)
 
     def y3(n, zt):
-        lo, size, _, fb_ = span(n)
-
         @pl.when(active)
         def _():
             for k in range(2):
-                wait(fb_.at[k], yfr.at[k, n])
-            at = pl.ds(lo, size)
-            o[other_e, zt, at] = o[other_e, zt, at] + (fb_[0] + fb_[1])
+                wait(yff.at[k, n], yfr.at[k, n])
+            at = pl.ds(0, FIRST)
+            o[other_e, zt, at] = o[other_e, zt, at] + (yff[0, n] + yff[1, n])
 
     def gview(e):
-        def view(zt, t, k):
-            return o.at[e, zt, pl.ds(FIRST + k * (REST // 2), REST // 2)] if t == 0 else o.at[e, zt, pl.ds(FIRST, REST)]
+        def view(zt, far, k):
+            return o.at[e, zt, pl.ds(FIRST + k * (REST // 2), REST // 2)] if far else o.at[e, zt, pl.ds(FIRST, REST)]
 
         return view
 
-    def fview(zt, t, k):
-        return o.at[other_e, zt, pl.ds(k * (FIRST // 2), FIRST // 2)] if t == 0 else o.at[other_e, zt, pl.ds(0, FIRST)]
+    def fview(zt, far, k):
+        return o.at[other_e, zt, pl.ds(k * (FIRST // 2), FIRST // 2)] if far else o.at[other_e, zt, pl.ds(0, FIRST)]
 
     def gland(e):
-        def land(t, k):
-            return gzb.at[e, k, t, pl.ds(0, REST // 2)] if t == 0 else gzb.at[e, k, t]
+        def land(i, k):
+            return gzb.at[e, k, i, pl.ds(0, REST // 2)] if G_HOPS[i][0] == 4 else gzb.at[e, k, i]
 
         return land
 
-    def fland(t, k):
-        return fzb.at[k, t, pl.ds(0, FIRST // 2)] if t == 0 else fzb.at[k, t]
-
-    def zsend(view, land, ssem, rsem, k, t):
-        zt = mod(z + (4 - t), NZ) if k == 0 else mod(z - (4 - t), NZ)
-        send(view(zt, t, k), land(t, k), ssem.at[k, t], rsem.at[k, t], z1=zp if k == 0 else zm)
-
-    def zrecv(view, land, rsem, k, t):
-        zt = mod(z + (3 - t), NZ) if k == 0 else mod(z - (3 - t), NZ)
-        wait(land(t, k), rsem.at[k, t])
-        into = view(zt, t, k)
-        into[...] = into[...] + land(t, k)[...]
-
-    def zwork(m, view, land, ssem, rsem):
-        if m == 0:
-            for k in range(2):
-                zsend(view, land, ssem, rsem, k, 0)
-        elif m < 7:
-            k, t = (0, (m - 1) // 2) if m % 2 else (1, m // 2 - 1)
-            zrecv(view, land, rsem, k, t)
-            zsend(view, land, ssem, rsem, k, t + 1)
-        else:
-            for k in range(2):
-                zrecv(view, land, rsem, k, 3)
-
-    def g(m):
-        for e in range(2):
-            zwork(m, gview(e), gland(e), gzs.at[e], gzr.at[e])
-
-    def f(m):
+    def fland(i, k):
+        return fzb.at[k, i, pl.ds(0, FIRST // 2)] if F_HOPS[i][0] == 4 else fzb.at[k, i]
+
+    def ahead(k, d):
+        return mod(z + d, NZ) if k == 0 else mod(z - d, NZ)
+
+    def ztake(view, land, rsem, hops, k, dist):
+        for i, (far, d) in enumerate(hops):
+            if d == dist:
+                wait(land(i, k), rsem.at[k, i])
+                into = view(ahead(k, d), far == 4, k)
+                into[...] = into[...] + land(i, k)[...]
+
+    def zpass(view, land, ssem, rsem, hops, k, i):
+        far, d = hops[i]
+        ztake(view, land, rsem, hops, k, far)
+        send(view(ahead(k, far), far == 4, k), land(i, k), ssem.at[k, i], rsem.at[k, i], z1=ahead(k, far - d))
+
+    def deliver(src, zt, slot_to, ssem, groups, z1, y1, local):
+        for i in groups:
+            x1, c1 = i // NC, i % NC
+            piece = src.at[zt, pl.ds(i * BLOCKS, BLOCKS)]
+            dst, rsem = fin.at[x, slot_to], finr.at[x, slot_to]
+            if local:
+
+                @pl.when(x * NC + c == i)
+                def _():
+                    pltpu.make_async_copy(piece, dst, rsem).start()
+
+                @pl.when(x * NC + c != i)
+                def _():
+                    send(piece, dst, ssem.at[i], rsem, z1=z1, x1=x1, c1=c1, y1=y1)
+            else:
+                send(piece, dst, ssem.at[i], rsem, z1=z1, x1=x1, c1=c1, y1=y1)
+
+    f_groups, g_groups = range(FIRST // BLOCKS), range(FIRST // BLOCKS, NX * NC)
+
+    def f_pass(k, i):
         @pl.when(active)
         def _():
-            zwork(m, fview, fland, fzs, fzr)
+            far, d = F_HOPS[i]
+            if d:
+                zpass(fview, fland, fzs, fzr, F_HOPS, k, i)
+            else:
+                ztake(fview, fland, fzr, F_HOPS, k, far)
+                j = k * len(F_LAST) + F_LAST.index(i)
+                deliver(o.at[other_e], ahead(k, far), 1 + j, ffs.at[j], f_groups, ahead(k, far), y, False)
+
+    def f_own():
+        @pl.when(active)
+        def _():
+            deliver(o.at[other_e], z, 0, fos, f_groups, z, y, True)
+
+    def g_last():
+        deliver(o.at[near_e], z, 1 + side, fns, g_groups, z, onward, False)
+
+        @pl.when(active)
+        def _():
+            deliver(o.at[other_e], z, 0, fos, g_groups, z, y, True)
+
+        @pl.when(jnp.logical_not(active))
+        def _():
+            deliver(o.at[other_e], z, 3, fos, g_groups, z, mod(y + 2, NY), False)
 
     def sent(n):
         z0 = mod(z + n, NZ)
@@ -398,73 +437,94 @@
             for d in (0, 1, -1, 2, -2, 3):
                 wait(ab.at[edge, z], azs.at[mod(z - d, NZ)])
 
-    order = [mod(z + d, NZ) for d in (4, 3, -3, 2, -2, 1, -1, 0)]
+    chunk = [mod(z + d, NZ) for d in (4, 3, -3, 2, -2, 1, -1, 0)]
+
+    def run(name, *a):
+        if name == "R":
+            residuals(chunk[a[0]])
+            sent(a[0])
+        elif name == "y1":
+            y1(a[0], chunk[a[0]])
+        elif name == "y2":
+            y2(a[0], chunk[a[0]])
+        elif name == "y3":
+            y3(a[0], chunk[a[0]])
+        elif name == "g":
+            e, k, i = a
+            zpass(gview(e), gland(e), gzs.at[e], gzr.at[e], G_HOPS, k, i)
+        elif name == "gr":
+            e, k = a
+            ztake(gview(e), gland(e), gzr.at[e], G_HOPS, k, 0)
+        elif name == "gfin":
+            g_last()
+        elif name == "f":
+            f_pass(*a)
+        elif name == "fown":
+            f_own()
+
+    for name, *a in ORDER:
+        run(name, *a)
+    sent_first()
+
     for n in range(NZ):
-        residuals(order[n])
-        y1(n, order[n])
-        if n >= 1:
-            y2(n - 1, order[n - 1])
-        if n < 7:
-            g(n)
-        if n >= 2:
-            y3(n - 2, order[n - 2])
-            f(n - 2)
-        sent(n)
-    sent_first()
-    y2(7, z)
-    y3(6, order[6])
-    f(6)
-    g(7)
-    y1(8, z)
-    y3(7, z)
-    y2(8, z)
-    f(7)
-    y3(8, z)
-
-    @pl.when(active)
-    def _():
-        fb[...] = o[other_e, z].astype(jnp.bfloat16)
-        for d in range(NX):
-            for e in range(NC):
-                x1, c1 = mod(x + d, NX), mod(c + e, NC)
-                src = fb.at[mine(x1, c1)]
-                dst = fr.at[:, pl.ds(pl.multiple_of(x * ROWS, ROWS), ROWS), :]
-                if d or e:
-                    send(src, dst, es.at[2 * d + e], er.at[x], x1=x1, c1=c1)
-                else:
-                    pltpu.make_async_copy(src, dst, er.at[x]).start()
-
-    for n in range(NZ + 1):
-        lo, size, hb, fb_ = span(n)
 
         @pl.when(jnp.logical_not(active))
         def _():
-            wait(hb, yhs.at[0, n])
-            wait(hb, yhs.at[1, n])
-
-        wait(fb_.at[0], yfs.at[n])
+            wait(yhf.at[n], yhs.at[0, n])
+            wait(yhf.at[n], yhs.at[1, n])
+
+        wait(yff.at[0, n], yfs.at[n])
     for k in range(2):
-        for t in range(4):
+        for i in range(len(G_HOPS)):
             for e in range(2):
-                wait(gland(e)(t, k), gzs.at[e, k, t])
+                wait(gland(e)(i, k), gzs.at[e, k, i])
+    piece = fin.at[0, 0]
 
     @pl.when(active)
     def _():
         for k in range(2):
-            for t in range(4):
-                wait(fland(t, k), fzs.at[k, t])
-        for n in range(1, NX * NC):
-            wait(fb.at[pl.ds(0, BLOCKS)], es.at[n])
-
-    for x0 in range(NX):
-        wait(fr.at[:, pl.ds(x0 * ROWS, ROWS), :], er.at[x0])
-    out[...] = fr[...]
+            for i in range(len(F_HOPS)):
+                if i not in F_LAST:
+                    wait(fland(i, k), fzs.at[k, i])
+        for j in range(2 * len(F_LAST)):
+            for i in f_groups:
+                wait(piece, ffs.at[j, i])
+        for i in f_groups:
+
+            @pl.when(x * NC + c != i)
+            def _():
+                wait(piece, fos.at[i])
+
+    for i in g_groups:
+        wait(piece, fns.at[i])
+
+        @pl.when(jnp.logical_or(jnp.logical_not(active), x * NC + c != i))
+        def _():
+            wait(piece, fos.at[i])
+
+    def collect(slots):
+        for x0 in range(NX):
+            for k in range(slots):
+                wait(fin.at[x0, k], finr.at[x0, k])
+            total = fin[x0, 0]
+            for k in range(1, slots):
+                total = total + fin[x0, k]
+            out[:, x0 * ROWS : (x0 + 1) * ROWS, :] = total.astype(jnp.bfloat16)
+
+    @pl.when(x * NC + c < FIRST // BLOCKS)
+    def _():
+        collect(1 + 2 * len(F_LAST))
+
+    @pl.when(x * NC + c >= FIRST // BLOCKS)
+    def _():
+        collect(4)
 
 
 def body(amplitudes, vectors, pair_count, tile_map):
     live = lax.broadcasted_iota(jnp.int32, (BLOCKS, 1, SLOTS), 2) < pair_count[:, None, None]
     f32, bf16 = jnp.float32, jnp.bfloat16
     dma = pltpu.SemaphoreType.DMA
+    slots = max(4, 1 + 2 * len(F_LAST))
     out = pl.pallas_call(
         kernel,
         out_shape=jax.ShapeDtypeStruct(amplitudes.shape, bf16),
@@ -489,10 +549,7 @@
             pltpu.VMEM((2, 4, FIRST, ROWS, SLOTS), f32),
             pltpu.VMEM((NZ, FIRST // 2, ROWS, SLOTS), f32),
             pltpu.VMEM((2, NZ, FIRST, ROWS, SLOTS), f32),
-            pltpu.VMEM((REST // 2, ROWS, SLOTS), f32),
-            pltpu.VMEM((2, REST, ROWS, SLOTS), f32),
-            pltpu.VMEM((GROUP, ROWS, SLOTS), bf16),
-            pltpu.VMEM((BLOCKS, NX * ROWS, SLOTS), bf16),
+            pltpu.VMEM((NX, slots, BLOCKS, ROWS, SLOTS), f32),
             dma((NZ,)), dma((NZ,)),
             dma((4, NZ)), dma((4, NZ)),
             dma((4, NZ)), dma((4, NZ)),
@@ -501,9 +558,10 @@
             dma((2, NZ)), dma((NZ,)), dma((3, NZ)),
             dma((2, 2, 4)), dma((2, 2, 4)),
             dma((2, 4)), dma((2, 4)),
-            dma((2, NZ + 1)), dma((NZ + 1,)),
-            dma((NZ + 1,)), dma((2, NZ + 1)),
-            dma((NX * NC,)), dma((NX,)),
+            dma((2, NZ)), dma((NZ,)),
+            dma((NZ,)), dma((2, NZ)),
+            dma((2 * len(F_LAST), NX * NC)), dma((NX * NC,)), dma((NX * NC,)),
+            dma((NX, slots)),
         ],
         compiler_params=pltpu.CompilerParams(
             collective_id=0, has_side_effects=True, vmem_limit_bytes=60 * 2**20

time: 116 us -> 112 us (0.966)
  Pallas kernels: 113 us -> 108 us
    pallas_call x1, Pallas kernels: 113 us -> 108 us  [body(): pl.pallas_call(kernel, out_shape=jax.ShapeDtypeStruct(amplitudes.shape, b...]
where the time goes in v6:
time: 112 us
  Pallas kernels  108 us (96%)
  other arithmetic  1.55 us (1%)
  local copies, waits for them, and re-layouts  1.51 us (1%)
    pallas_call x1, Pallas kernels, body(): pl.pallas_call(kernel, out_shape=jax.ShapeDtypeStruct(amplitudes.shape, b...  108 us

profile of v6, /device:TPU:1, one launch (start us, length us, event | category | flops | bytes accessed | tf_op | source)
XLA Modules:
  0.0 111.6 jit_solution(14676249323750952663)
XLA Ops:
  0.0 1.5 %copy.5.tiles = s32[256,32]{1,0:T(8,128)} copy(s32[256,32]{0,1:T(8,128)} %param.7) | data formatting | bytes 65536 | tf_op args[3]
  1.5 0.0 copy-start
  1.5 108.5 %shard_map.46 = bf16[4,64,128]{2,1,0:T(8,128)(2,1)} custom-call(bf16[4,64,128]{2,1,0:T(8,128)(2,1)} %amp_in.1, bf16[4,1280,128]{2,1,0:T(8,128)(2,1)} %vec.1, s32[4]{0:T(128)} %counts.1, s32[256,32]{1,0:T(8,128)} %copy.5.tiles), custom_call_target="tpu_custom_call" | custom-call | flops 12000000000 | bytes 4000000 | tf_op jit(solution)/shard_map/pallas_call | solution.py:528
  110.0 0.0 copy-done
  110.0 0.1 iota_compare_fusion
  110.1 1.5 %broadcast_select_fusion = bf16[4,64,128]{2,1,0:T(8,128)(2,1)} fusion(bf16[4,64,128]{2,1,0:T(8,128)(2,1)} %shard_map.46, pred[4,128]{1,0:T(4,128)(4,1)S(1)} %iota_compare_fusion), kind=kLoop, calls=%fused_computation | loop fusion | flops 32768 | bytes 131584 | tf_op jit(solution)/shard_map/jit(_where)/select_n | solution.py:571
Async XLA Ops:
  1.5 108.5 %copy-start = (s32[4]{0:T(128)S(1)}, s32[4]{0:T(128)}, u32[]{:S(2)}) copy-start(s32[4]{0:T(128)} %counts.1) | copy-start | bytes 52

commit v7 on v6

--- a/solution.py
+++ b/solution.py
@@ -174,7 +174,7 @@
                 dst[to, :] = dst[to, :] + part_sum if half else part_sum
             return carry
 
-        lax.fori_loop(0, src.shape[0] // PITCH // 2, some, 0)
+        lax.fori_loop(0, src.shape[0] // PITCH // 2, some, 0, unroll=4)
 
     def spread(z0):
         block = vb.at[z0, mine(x, c)]
@@ -300,7 +300,7 @@
                 o[1, zt, p] = r[ROWS:]
             return carry
 
-        lax.fori_loop(0, GROUP // 4, some, 0)
+        lax.fori_loop(0, GROUP // 4, some, 0, unroll=2)
 
     def y1(n, zt):
         @pl.when(jnp.logical_not(active))

time: 112 us -> 107 us (0.955)
  Pallas kernels: 108 us -> 104 us
    pallas_call x1, Pallas kernels: 108 us -> 104 us  [body(): pl.pallas_call(kernel, out_shape=jax.ShapeDtypeStruct(amplitudes.shape, b...]
where the time goes in v7:
time: 107 us
  Pallas kernels  104 us (97%)
  other arithmetic  1.55 us (1%)
  local copies, waits for them, and re-layouts  1.51 us (1%)
    pallas_call x1, Pallas kernels, body(): pl.pallas_call(kernel, out_shape=jax.ShapeDtypeStruct(amplitudes.shape, b...  104 us

profile of v7, /device:TPU:1, one launch (start us, length us, event | category | flops | bytes accessed | tf_op | source)
XLA Modules:
  0.0 106.6 jit_solution(937155883273824203)
XLA Ops:
  0.0 1.5 %copy.5.tiles = s32[256,32]{1,0:T(8,128)} copy(s32[256,32]{0,1:T(8,128)} %param.7) | data formatting | bytes 65536 | tf_op args[3]
  1.5 0.0 copy-start
  1.5 103.5 %shard_map.46 = bf16[4,64,128]{2,1,0:T(8,128)(2,1)} custom-call(bf16[4,64,128]{2,1,0:T(8,128)(2,1)} %amp_in.1, bf16[4,1280,128]{2,1,0:T(8,128)(2,1)} %vec.1, s32[4]{0:T(128)} %counts.1, s32[256,32]{1,0:T(8,128)} %copy.5.tiles), custom_call_target="tpu_custom_call" | custom-call | flops 12000000000 | bytes 4000000 | tf_op jit(solution)/shard_map/pallas_call | solution.py:528
  105.0 0.0 copy-done
  105.0 0.1 iota_compare_fusion
  105.1 1.5 %broadcast_select_fusion = bf16[4,64,128]{2,1,0:T(8,128)(2,1)} fusion(bf16[4,64,128]{2,1,0:T(8,128)(2,1)} %shard_map.46, pred[4,128]{1,0:T(4,128)(4,1)S(1)} %iota_compare_fusion), kind=kLoop, calls=%fused_computation | loop fusion | flops 32768 | bytes 131584 | tf_op jit(solution)/shard_map/jit(_where)/select_n | solution.py:571
Async XLA Ops:
  1.5 103.5 %copy-start = (s32[4]{0:T(128)S(1)}, s32[4]{0:T(128)}, u32[]{:S(2)}) copy-start(s32[4]{0:T(128)} %counts.1) | copy-start | bytes 52

commit v8 on v7

--- a/solution.py
+++ b/solution.py
@@ -23,14 +23,14 @@
 ORDER = (
     ("R", 0), ("g", 0, 0, 0), ("g", 0, 1, 0), ("g", 1, 0, 0), ("g", 1, 1, 0), ("y1", 0),
     ("R", 1), ("g", 0, 0, 1), ("g", 1, 0, 1), ("y1", 1), ("R", 2), ("g", 0, 1, 1),
-    ("g", 1, 1, 1), ("y1", 2), ("R", 3), ("y2", 0), ("y1", 3), ("R", 4),
-    ("y2", 1), ("y1", 4), ("R", 5), ("g", 0, 0, 2), ("g", 0, 1, 2), ("y2", 2),
-    ("y1", 5), ("R", 6), ("g", 1, 0, 2), ("g", 1, 1, 2), ("y3", 0), ("f", 0, 0),
-    ("f", 1, 0), ("y2", 3), ("y1", 6), ("R", 7), ("y3", 1), ("f", 0, 1),
-    ("g", 0, 0, 3), ("g", 0, 1, 3), ("y2", 4), ("y1", 7), ("y3", 2), ("f", 1, 1),
-    ("y2", 5), ("g", 1, 0, 3), ("g", 1, 1, 3), ("y3", 3), ("y2", 6), ("f", 0, 2),
-    ("gr", 0, 1), ("y3", 4), ("y2", 7), ("gr", 0, 0), ("f", 1, 2), ("y3", 5),
-    ("f", 0, 3), ("gr", 1, 0), ("gr", 1, 1), ("gfin",), ("y3", 6), ("f", 1, 3),
+    ("g", 1, 1, 1), ("y1", 2), ("R", 3), ("y1", 3), ("R", 4), ("y2", 0),
+    ("y1", 4), ("R", 5), ("y2", 1), ("y1", 5), ("R", 6), ("y2", 2),
+    ("y2", 3), ("y1", 6), ("R", 7), ("g", 0, 0, 2), ("g", 0, 1, 2), ("y1", 7),
+    ("y3", 0), ("f", 0, 0), ("f", 1, 0), ("y2", 4), ("g", 1, 0, 2), ("g", 1, 1, 2),
+    ("y3", 1), ("f", 0, 1), ("y2", 5), ("g", 0, 0, 3), ("g", 0, 1, 3), ("y3", 2),
+    ("f", 1, 1), ("y3", 3), ("y2", 6), ("g", 1, 0, 3), ("g", 1, 1, 3), ("y2", 7),
+    ("f", 0, 2), ("y3", 4), ("gr", 0, 1), ("gr", 0, 0), ("f", 1, 2), ("y3", 5),
+    ("f", 0, 3), ("y3", 6), ("f", 1, 3), ("gr", 1, 0), ("gr", 1, 1), ("gfin",),
     ("y3", 7), ("fown",),
 )
 
@@ -102,21 +102,22 @@
     for b in range(BLOCKS):
         amp[b] = jnp.where(slot < counts[b], amp_in[b], jnp.zeros_like(amp_in[b]))
 
-    column = lax.broadcasted_iota(jnp.int32, (32, TOTAL), 1)
-    block_of = source(lax.div(column, GROUP)) * GROUP + lax.rem(column, GROUP)
+    block_row = lax.broadcasted_iota(jnp.int32, (GROUP, TOTAL), 0)
 
     def adjacency(n, carry):
-        at = pl.ds(pl.multiple_of(n * 32, 32), 32)
-        named = tiles[at, :]
-        found = jnp.zeros((32, TOTAL), jnp.float32)
-        for j in range(tiles.shape[1]):
-            found = found + jnp.where(named[:, j : j + 1] == block_of, 1.0, 0.0)
-        found = found.astype(jnp.bfloat16)
+        block_of = block_row + source(n) * GROUP
+        found = jnp.zeros((GROUP, TOTAL), jnp.float32)
+        for j in range(tiles.shape[0]):
+            found = found + jnp.where(tiles[j : j + 1, :] == block_of, 1.0, 0.0)
+        for h in range(2):
+            u[pl.ds(pl.multiple_of(h * TOTAL + n * GROUP, GROUP), GROUP), :] = found[:, h * SLOTS : (h + 1) * SLOTS]
+        return carry
+
+    lax.fori_loop(0, NZ, adjacency, 0)
+    for h in range(2):
+        found = u[h * TOTAL : (h + 1) * TOTAL, :].T.astype(jnp.bfloat16)
         for k in range(4):
-            near[at, k * SLOTS : (k + 1) * SLOTS] = found[:, k // 2 * SLOTS : (k // 2 + 1) * SLOTS]
-        return carry
-
-    lax.fori_loop(0, TOTAL // 32, adjacency, 0)
+            near[h * SLOTS : (h + 1) * SLOTS, k * SLOTS : (k + 1) * SLOTS] = found[:, k // 2 * SLOTS : (k // 2 + 1) * SLOTS]
     pl.semaphore_wait(barrier, NZ - 1 + NX * NC - 1 + NY - 1)
 
     for d in range(NX):
@@ -178,8 +179,11 @@
 
     def spread(z0):
         block = vb.at[z0, mine(x, c)]
-        send(block, block, xs.at[0, z0], xr.at[0, z0], x1=xp)
-        send(block, block, xs.at[1, z0], xr.at[1, z0], x1=xm)
+        ha, hb = vb.at[z0, part(x, c, 0)], vb.at[z0, part(x, c, 1)]
+        send(ha, ha, xs.at[0, z0], xr.at[0, z0], x1=xp)
+        send(hb, hb, xs.at[1, z0], xr.at[1, z0], x1=xm)
+        send(hb, hb, xs.at[4, z0], xr.at[4, z0], x1=xp)
+        send(ha, ha, xs.at[5, z0], xr.at[5, z0], x1=xm)
         send(block, block, ss.at[0, z0], sr.at[0, z0], c1=mate)
 
     wait(vb.at[z, mine(x, c)], vzr.at[z])
@@ -233,18 +237,25 @@
         def _():
             z0 = source(s - 1)
             left, right = vb.at[z0, mine(xm, c)], vb.at[z0, mine(xp, c)]
-            wait(left, xr.at[0, z0])
             half = vb.at[z0, part(xm, c, 0)]
+            wait(half, xr.at[0, z0])
             send(half, half, xs.at[2, z0], xr.at[2, z0], x1=xp)
+            half = vb.at[z0, part(xp, c, 1)]
+            wait(half, xr.at[1, z0])
+            send(half, half, xs.at[3, z0], xr.at[3, z0], x1=xm)
+            wait(vb.at[z0, part(xm, c, 1)], xr.at[4, z0])
             send(left, left, ss.at[1, z0], sr.at[1, z0], c1=mate)
-            wait(right, xr.at[1, z0])
-            half = vb.at[z0, part(xp, c, 1)]
-            send(half, half, xs.at[3, z0], xr.at[3, z0], x1=xm)
+            wait(vb.at[z0, part(xp, c, 0)], xr.at[5, z0])
             send(right, right, ss.at[2, z0], sr.at[2, z0], c1=mate)
 
         @pl.when(jnp.logical_and(s >= 2, s < NZ + 2))
         def _():
             z0 = source(s - 2)
+
+            wait(vb.at[z0, part(xo, c, 0)], xr.at[2, z0])
+            wait(vb.at[z0, part(xo, c, 1)], xr.at[3, z0])
+            block = vb.at[z0, mine(xo, c)]
+            send(block, block, ss.at[3, z0], sr.at[3, z0], c1=mate)
 
             @pl.when(jnp.logical_not(active))
             def _():
@@ -255,10 +266,6 @@
                 products(s - 2, z0, x0, c)
             wait(vb.at[z0, mine(x, mate)], sr.at[0, z0])
             products(s - 2, z0, x, mate)
-            wait(vb.at[z0, part(xo, c, 0)], xr.at[2, z0])
-            wait(vb.at[z0, part(xo, c, 1)], xr.at[3, z0])
-            block = vb.at[z0, mine(xo, c)]
-            send(block, block, ss.at[3, z0], sr.at[3, z0], c1=mate)
             products(s - 2, z0, xo, c)
             for k, x0 in ((1, xm), (2, xp)):
                 wait(vb.at[z0, mine(x0, mate)], sr.at[k, z0])
@@ -405,9 +412,8 @@
     def sent(n):
         z0 = mod(z + n, NZ)
         block, half = vb.at[z0, mine(x, c)], vb.at[z0, part(x, c, 0)]
-        for k in range(2):
-            wait(block, xs.at[k, z0])
-            wait(half, xs.at[2 + k, z0])
+        for k in range(6):
+            wait(half, xs.at[k, z0])
         for k in range(4):
             wait(block, ss.at[k, z0])
 
@@ -551,7 +557,7 @@
             pltpu.VMEM((2, NZ, FIRST, ROWS, SLOTS), f32),
             pltpu.VMEM((NX, slots, BLOCKS, ROWS, SLOTS), f32),
             dma((NZ,)), dma((NZ,)),
-            dma((4, NZ)), dma((4, NZ)),
+            dma((6, NZ)), dma((6, NZ)),
             dma((4, NZ)), dma((4, NZ)),
             dma((NX,)), dma((NX, NC)),
             dma((NZ + 1,)), dma((NZ,)),
@@ -567,7 +573,7 @@
             collective_id=0, has_side_effects=True, vmem_limit_bytes=60 * 2**20
         ),
         cost_estimate=pl.CostEstimate(flops=12 * 10**9, bytes_accessed=4 * 10**6, transcendentals=0),
-    )(amplitudes, vectors, pair_count, tile_map)
+    )(amplitudes, vectors, pair_count, tile_map.T)
     return jnp.where(live, out, jnp.zeros_like(out))
 
 

time: 107 us -> 104 us (0.972)
  Pallas kernels: 104 us -> 102 us
  local copies, waits for them, and re-layouts: 1.51 us -> 0 us
    unnamed x3 -> x0, local copies, waits for them, and re-layouts: 1.51 us -> none
    pallas_call x1, Pallas kernels: 104 us -> 102 us  [body(): pl.pallas_call(kernel, out_shape=jax.ShapeDtypeStruct(amplitudes.shape, b...]
where the time goes in v8:
time: 104 us
  Pallas kernels  102 us (98%)
  other arithmetic  2.2 us (2%)
    pallas_call x1, Pallas kernels, body(): pl.pallas_call(kernel, out_shape=jax.ShapeDtypeStruct(amplitudes.shape, b...  102 us

profile of v8, /device:TPU:1, one launch (start us, length us, event | category | flops | bytes accessed | tf_op | source)
XLA Modules:
  0.0 104.2 jit_solution(12615488445192965283)
XLA Ops:
  0.0 0.7 iota_compare_fusion
  0.7 102.0 %shard_map.46 = bf16[4,64,128]{2,1,0:T(8,128)(2,1)} custom-call(bf16[4,64,128]{2,1,0:T(8,128)(2,1)} %amp_in.1, bf16[4,1280,128]{2,1,0:T(8,128)(2,1)} %vec.1, s32[4]{0:T(128)} %counts.1, s32[32,256]{1,0:T(8,128)} %bitcast.1), custom_call_target="tpu_custom_call" | custom-call | flops 12000000000 | bytes 4000000 | tf_op jit(solution)/shard_map/pallas_call | solution.py:534
  102.7 1.5 %broadcast_select_fusion = bf16[4,64,128]{2,1,0:T(8,128)(2,1)} fusion(bf16[4,64,128]{2,1,0:T(8,128)(2,1)} %shard_map.46, pred[4,128]{1,0:T(4,128)(4,1)S(1)} %iota_compare_fusion), kind=kLoop, calls=%fused_computation | loop fusion | flops 32768 | bytes 131584 | tf_op jit(solution)/shard_map/jit(_where)/select_n | solution.py:577

commit v9 on v8

--- a/solution.py
+++ b/solution.py
@@ -25,12 +25,12 @@
     ("R", 1), ("g", 0, 0, 1), ("g", 1, 0, 1), ("y1", 1), ("R", 2), ("g", 0, 1, 1),
     ("g", 1, 1, 1), ("y1", 2), ("R", 3), ("y1", 3), ("R", 4), ("y2", 0),
     ("y1", 4), ("R", 5), ("y2", 1), ("y1", 5), ("R", 6), ("y2", 2),
-    ("y2", 3), ("y1", 6), ("R", 7), ("g", 0, 0, 2), ("g", 0, 1, 2), ("y1", 7),
+    ("y1", 6), ("R", 7), ("y2", 3), ("y1", 7), ("g", 0, 0, 2), ("g", 0, 1, 2),
     ("y3", 0), ("f", 0, 0), ("f", 1, 0), ("y2", 4), ("g", 1, 0, 2), ("g", 1, 1, 2),
     ("y3", 1), ("f", 0, 1), ("y2", 5), ("g", 0, 0, 3), ("g", 0, 1, 3), ("y3", 2),
-    ("f", 1, 1), ("y3", 3), ("y2", 6), ("g", 1, 0, 3), ("g", 1, 1, 3), ("y2", 7),
-    ("f", 0, 2), ("y3", 4), ("gr", 0, 1), ("gr", 0, 0), ("f", 1, 2), ("y3", 5),
-    ("f", 0, 3), ("y3", 6), ("f", 1, 3), ("gr", 1, 0), ("gr", 1, 1), ("gfin",),
+    ("f", 1, 1), ("y2", 6), ("y3", 3), ("g", 1, 0, 3), ("g", 1, 1, 3), ("y2", 7),
+    ("f", 0, 2), ("y3", 4), ("gr", 0, 1), ("y3", 5), ("f", 0, 3), ("f", 1, 2),
+    ("gr", 0, 0), ("y3", 6), ("f", 1, 3), ("gr", 1, 0), ("gr", 1, 1), ("gfin",),
     ("y3", 7), ("fown",),
 )
 
@@ -45,10 +45,10 @@
 
 
 def kernel(
-    amp_in, vec, counts, tiles, out,
-    amp, near, vb, ab, w, wt, u, ut, o, gzb, fzb, yhf, yff, fin,
+    amp_in, vec, counts, tiles_in, out,
+    amp, tiles, near, vb, ab, w, wt, u, ut, o, gzb, fzb, yhf, yff, fin,
     vzs, vzr, xs, xr, ss, sr, axs, axr, azs, azr, ays, ayf, ayr,
-    gzs, gzr, fzs, fzr, yhs, yhr, yfs, yfr, ffs, fos, fns, finr,
+    gzs, gzr, fzs, fzr, yhs, yhr, yfs, yfr, ffs, fos, fns, finr, loads,
 ):
     z, x, c, y = (lax.axis_index(a) for a in ("z", "x", "c", "y"))
 
@@ -84,7 +84,11 @@
         return pl.ds(pl.multiple_of(z1 * DEPTH, DEPTH), DEPTH)
 
     own = pltpu.make_async_copy(vec.at[:, rows(z), :], vb.at[z, mine(x, c)], vzr.at[z])
+    load_amp = pltpu.make_async_copy(amp_in, amp, loads.at[0])
+    load_amp.start()
     own.start()
+    load_tiles = pltpu.make_async_copy(tiles_in, tiles, loads.at[1])
+    load_tiles.start()
     barrier = pltpu.get_barrier_semaphore()
     slot = lax.broadcasted_iota(jnp.int32, (NX * ROWS, SLOTS), 1)
 
@@ -99,10 +103,12 @@
                 greet(x1=mod(x + d, NX), c1=mod(c + e, NC))
     for d in range(1, NY):
         greet(y1=mod(y + d, NY))
+    load_amp.wait()
     for b in range(BLOCKS):
-        amp[b] = jnp.where(slot < counts[b], amp_in[b], jnp.zeros_like(amp_in[b]))
-
+        amp[b] = jnp.where(slot < counts[b], amp[b], jnp.zeros_like(amp[b]))
     block_row = lax.broadcasted_iota(jnp.int32, (GROUP, TOTAL), 0)
+
+    load_tiles.wait()
 
     def adjacency(n, carry):
         block_of = block_row + source(n) * GROUP
@@ -175,7 +181,7 @@
                 dst[to, :] = dst[to, :] + part_sum if half else part_sum
             return carry
 
-        lax.fori_loop(0, src.shape[0] // PITCH // 2, some, 0, unroll=4)
+        lax.fori_loop(0, src.shape[0] // PITCH // 2, some, 0, unroll=8 if src.shape[0] == 2 * ROWS * PITCH else 4)
 
     def spread(z0):
         block = vb.at[z0, mine(x, c)]
@@ -188,6 +194,14 @@
 
     wait(vb.at[z, mine(x, c)], vzr.at[z])
     spread(z)
+
+    def hand_first():
+        for n in range(1, AHEAD + 1):
+            hand_out(jnp.int32(n))
+
+    @pl.when(jnp.logical_not(active))
+    def _():
+        hand_first()
 
     @pl.when(active)
     def _():
@@ -198,9 +212,7 @@
         send(block, block, azs.at[z], azr.at[z], z1=zp)
         send(block, block, azs.at[NZ], azr.at[z], z1=zm)
         spread_amp(z)
-
-    for s in range(1, AHEAD + 1):
-        hand_out(jnp.int32(s))
+        hand_first()
 
     def step(s, carry):
         @pl.when(jnp.logical_and(jnp.logical_and(s >= 1, s < NZ), active))
@@ -535,14 +547,15 @@
         kernel,
         out_shape=jax.ShapeDtypeStruct(amplitudes.shape, bf16),
         in_specs=[
-            pl.BlockSpec(memory_space=pltpu.VMEM),
+            pl.BlockSpec(memory_space=pl.ANY),
             pl.BlockSpec(memory_space=pl.ANY),
             pl.BlockSpec(memory_space=pltpu.SMEM),
-            pl.BlockSpec(memory_space=pltpu.VMEM),
+            pl.BlockSpec(memory_space=pl.ANY),
         ],
         out_specs=pl.BlockSpec(memory_space=pltpu.VMEM),
         scratch_shapes=[
             pltpu.VMEM(amplitudes.shape, bf16),
+            pltpu.VMEM(tile_map.shape[::-1], jnp.int32),
             pltpu.VMEM((TOTAL, 2 * TOTAL), bf16),
             pltpu.VMEM((NZ, GROUP, DEPTH, SLOTS), bf16),
             pltpu.VMEM((2, NZ, GROUP, ROWS, SLOTS), bf16),
@@ -568,6 +581,7 @@
             dma((NZ,)), dma((2, NZ)),
             dma((2 * len(F_LAST), NX * NC)), dma((NX * NC,)), dma((NX * NC,)),
             dma((NX, slots)),
+            dma((2,)),
         ],
         compiler_params=pltpu.CompilerParams(
             collective_id=0, has_side_effects=True, vmem_limit_bytes=60 * 2**20

time: 104 us -> 103 us (level)
    pallas_call x1, Pallas kernels: 102 us -> 101 us  [body(): pl.pallas_call(kernel, out_shape=jax.ShapeDtypeStruct(amplitudes.shape, b...]
where the time goes in v9:
time: 103 us
  Pallas kernels  101 us (98%)
  other arithmetic  2.2 us (2%)
    pallas_call x1, Pallas kernels, body(): pl.pallas_call(kernel, out_shape=jax.ShapeDtypeStruct(amplitudes.shape, b...  101 us

profile of v9, /device:TPU:1, one launch (start us, length us, event | category | flops | bytes accessed | tf_op | source)
XLA Modules:
  0.0 102.8 jit_solution(3294207379089763545)
XLA Ops:
  0.0 0.7 iota_compare_fusion
  0.7 100.6 %shard_map.46 = bf16[4,64,128]{2,1,0:T(8,128)(2,1)} custom-call(bf16[4,64,128]{2,1,0:T(8,128)(2,1)} %amp_in.1, bf16[4,1280,128]{2,1,0:T(8,128)(2,1)} %vec.1, s32[4]{0:T(128)} %counts.1, s32[32,256]{1,0:T(8,128)} %bitcast.1), custom_call_target="tpu_custom_call" | custom-call | flops 12000000000 | bytes 4000000 | tf_op jit(solution)/shard_map/pallas_call | solution.py:546
  101.3 1.5 %broadcast_select_fusion = bf16[4,64,128]{2,1,0:T(8,128)(2,1)} fusion(bf16[4,64,128]{2,1,0:T(8,128)(2,1)} %shard_map.46, pred[4,128]{1,0:T(4,128)(4,1)S(1)} %iota_compare_fusion), kind=kLoop, calls=%fused_computation | loop fusion | flops 32768 | bytes 131584 | tf_op jit(solution)/shard_map/jit(_where)/select_n | solution.py:591

commit v10 on v9

--- a/solution.py
+++ b/solution.py
@@ -181,7 +181,7 @@
                 dst[to, :] = dst[to, :] + part_sum if half else part_sum
             return carry
 
-        lax.fori_loop(0, src.shape[0] // PITCH // 2, some, 0, unroll=8 if src.shape[0] == 2 * ROWS * PITCH else 4)
+        lax.fori_loop(0, src.shape[0] // PITCH // 2, some, 0, unroll=True)
 
     def spread(z0):
         block = vb.at[z0, mine(x, c)]
@@ -559,10 +559,10 @@
             pltpu.VMEM((TOTAL, 2 * TOTAL), bf16),
             pltpu.VMEM((NZ, GROUP, DEPTH, SLOTS), bf16),
             pltpu.VMEM((2, NZ, GROUP, ROWS, SLOTS), bf16),
-            pltpu.VMEM((2 * ROWS * PITCH, SLOTS), f32),
-            pltpu.VMEM((8 * PITCH, SLOTS), f32),
-            pltpu.VMEM((2 * ROWS * PITCH, SLOTS), f32),
-            pltpu.VMEM((8 * PITCH, SLOTS), f32),
+            pltpu.VMEM(((2 * ROWS + 1) * PITCH, SLOTS), f32),
+            pltpu.VMEM((9 * PITCH, SLOTS), f32),
+            pltpu.VMEM(((2 * ROWS + 1) * PITCH, SLOTS), f32),
+            pltpu.VMEM((9 * PITCH, SLOTS), f32),
             pltpu.VMEM((2, NZ, GROUP, ROWS, SLOTS), f32),
             pltpu.VMEM((2, 2, 4, REST, ROWS, SLOTS), f32),
             pltpu.VMEM((2, 4, FIRST, ROWS, SLOTS), f32),

time: 103 us -> 103 us (level)
  no operation moved by 1% of the time
where the time goes in v10:
time: 103 us; the launch traced here: 102 us
  Pallas kernels  100 us (97%)
  other arithmetic  2.2 us (2%)
    pallas_call x1, Pallas kernels, body(): pl.pallas_call(kernel, out_shape=jax.ShapeDtypeStruct(amplitudes.shape, b...  100 us

profile of v10, /device:TPU:1, one launch (start us, length us, event | category | flops | bytes accessed | tf_op | source)
XLA Modules:
  0.0 102.4 jit_solution(11574464831141681832)
XLA Ops:
  0.0 0.7 iota_compare_fusion
  0.7 100.2 %shard_map.46 = bf16[4,64,128]{2,1,0:T(8,128)(2,1)} custom-call(bf16[4,64,128]{2,1,0:T(8,128)(2,1)} %amp_in.1, bf16[4,1280,128]{2,1,0:T(8,128)(2,1)} %vec.1, s32[4]{0:T(128)} %counts.1, s32[32,256]{1,0:T(8,128)} %bitcast.1), custom_call_target="tpu_custom_call" | custom-call | flops 12000000000 | bytes 4000000 | tf_op jit(solution)/shard_map/pallas_call | solution.py:546
  100.9 1.5 %broadcast_select_fusion = bf16[4,64,128]{2,1,0:T(8,128)(2,1)} fusion(bf16[4,64,128]{2,1,0:T(8,128)(2,1)} %shard_map.46, pred[4,128]{1,0:T(4,128)(4,1)S(1)} %iota_compare_fusion), kind=kLoop, calls=%fused_computation | loop fusion | flops 32768 | bytes 131584 | tf_op jit(solution)/shard_map/jit(_where)/select_n | solution.py:591

commit v11 on v10

--- a/solution.py
+++ b/solution.py
@@ -25,13 +25,12 @@
     ("R", 1), ("g", 0, 0, 1), ("g", 1, 0, 1), ("y1", 1), ("R", 2), ("g", 0, 1, 1),
     ("g", 1, 1, 1), ("y1", 2), ("R", 3), ("y1", 3), ("R", 4), ("y2", 0),
     ("y1", 4), ("R", 5), ("y2", 1), ("y1", 5), ("R", 6), ("y2", 2),
-    ("y1", 6), ("R", 7), ("y2", 3), ("y1", 7), ("g", 0, 0, 2), ("g", 0, 1, 2),
+    ("y1", 6), ("R", 7), ("y2", 3), ("f7",), ("g", 0, 0, 2), ("g", 0, 1, 2),
     ("y3", 0), ("f", 0, 0), ("f", 1, 0), ("y2", 4), ("g", 1, 0, 2), ("g", 1, 1, 2),
     ("y3", 1), ("f", 0, 1), ("y2", 5), ("g", 0, 0, 3), ("g", 0, 1, 3), ("y3", 2),
-    ("f", 1, 1), ("y2", 6), ("y3", 3), ("g", 1, 0, 3), ("g", 1, 1, 3), ("y2", 7),
-    ("f", 0, 2), ("y3", 4), ("gr", 0, 1), ("y3", 5), ("f", 0, 3), ("f", 1, 2),
-    ("gr", 0, 0), ("y3", 6), ("f", 1, 3), ("gr", 1, 0), ("gr", 1, 1), ("gfin",),
-    ("y3", 7), ("fown",),
+    ("f", 1, 1), ("y2", 6), ("y3", 3), ("g", 1, 0, 3), ("g", 1, 1, 3), ("f", 0, 2),
+    ("gr", 0, 1), ("gr", 0, 0), ("y3", 4), ("f", 1, 2), ("gr", 1, 0), ("gr", 1, 1),
+    ("gfin",), ("y3", 5), ("f", 0, 3), ("y3", 6), ("f", 1, 3),
 )
 
 
@@ -405,21 +404,16 @@
                 j = k * len(F_LAST) + F_LAST.index(i)
                 deliver(o.at[other_e], ahead(k, far), 1 + j, ffs.at[j], f_groups, ahead(k, far), y, False)
 
-    def f_own():
+    def last(groups, base):
+        deliver(o.at[near_e], z, base + side, fns, groups, z, onward, False)
+
         @pl.when(active)
         def _():
-            deliver(o.at[other_e], z, 0, fos, f_groups, z, y, True)
-
-    def g_last():
-        deliver(o.at[near_e], z, 1 + side, fns, g_groups, z, onward, False)
-
-        @pl.when(active)
-        def _():
-            deliver(o.at[other_e], z, 0, fos, g_groups, z, y, True)
+            deliver(o.at[other_e], z, 0, fos, groups, z, y, True)
 
         @pl.when(jnp.logical_not(active))
         def _():
-            deliver(o.at[other_e], z, 3, fos, g_groups, z, mod(y + 2, NY), False)
+            deliver(o.at[other_e], z, base + 2, fos, groups, z, mod(y + 2, NY), False)
 
     def sent(n):
         z0 = mod(z + n, NZ)
@@ -474,17 +468,17 @@
             e, k = a
             ztake(gview(e), gland(e), gzr.at[e], G_HOPS, k, 0)
         elif name == "gfin":
-            g_last()
+            last(g_groups, 1)
         elif name == "f":
             f_pass(*a)
-        elif name == "fown":
-            f_own()
+        elif name == "f7":
+            last(f_groups, 1 + 2 * len(F_LAST))
 
     for name, *a in ORDER:
         run(name, *a)
     sent_first()
 
-    for n in range(NZ):
+    for n in range(NZ - 1):
 
         @pl.when(jnp.logical_not(active))
         def _():
@@ -507,13 +501,8 @@
         for j in range(2 * len(F_LAST)):
             for i in f_groups:
                 wait(piece, ffs.at[j, i])
-        for i in f_groups:
-
-            @pl.when(x * NC + c != i)
-            def _():
-                wait(piece, fos.at[i])
-
-    for i in g_groups:
+
+    for i in range(NX * NC):
         wait(piece, fns.at[i])
 
         @pl.when(jnp.logical_or(jnp.logical_not(active), x * NC + c != i))
@@ -531,7 +520,7 @@
 
     @pl.when(x * NC + c < FIRST // BLOCKS)
     def _():
-        collect(1 + 2 * len(F_LAST))
+        collect(4 + 2 * len(F_LAST))
 
     @pl.when(x * NC + c >= FIRST // BLOCKS)
     def _():
@@ -542,7 +531,7 @@
     live = lax.broadcasted_iota(jnp.int32, (BLOCKS, 1, SLOTS), 2) < pair_count[:, None, None]
     f32, bf16 = jnp.float32, jnp.bfloat16
     dma = pltpu.SemaphoreType.DMA
-    slots = max(4, 1 + 2 * len(F_LAST))
+    slots = 4 + 2 * len(F_LAST)
     out = pl.pallas_call(
         kernel,
         out_shape=jax.ShapeDtypeStruct(amplitudes.shape, bf16),
@@ -566,8 +555,8 @@
             pltpu.VMEM((2, NZ, GROUP, ROWS, SLOTS), f32),
             pltpu.VMEM((2, 2, 4, REST, ROWS, SLOTS), f32),
             pltpu.VMEM((2, 4, FIRST, ROWS, SLOTS), f32),
-            pltpu.VMEM((NZ, FIRST // 2, ROWS, SLOTS), f32),
-            pltpu.VMEM((2, NZ, FIRST, ROWS, SLOTS), f32),
+            pltpu.VMEM((NZ - 1, FIRST // 2, ROWS, SLOTS), f32),
+            pltpu.VMEM((2, NZ - 1, FIRST, ROWS, SLOTS), f32),
             pltpu.VMEM((NX, slots, BLOCKS, ROWS, SLOTS), f32),
             dma((NZ,)), dma((NZ,)),
             dma((6, NZ)), dma((6, NZ)),
@@ -577,8 +566,8 @@
             dma((2, NZ)), dma((NZ,)), dma((3, NZ)),
             dma((2, 2, 4)), dma((2, 2, 4)),
             dma((2, 4)), dma((2, 4)),
-            dma((2, NZ)), dma((NZ,)),
-            dma((NZ,)), dma((2, NZ)),
+            dma((2, NZ - 1)), dma((NZ - 1,)),
+            dma((NZ - 1,)), dma((2, NZ - 1)),
             dma((2 * len(F_LAST), NX * NC)), dma((NX * NC,)), dma((NX * NC,)),
             dma((NX, slots)),
             dma((2,)),

time: 103 us -> 103 us (level)
  no operation moved by 1% of the time
where the time goes in v11:
time: 103 us
  Pallas kernels  101 us (98%)
  other arithmetic  2.2 us (2%)
    pallas_call x1, Pallas kernels, body(): pl.pallas_call(kernel, out_shape=jax.ShapeDtypeStruct(amplitudes.shape, b...  101 us

profile of v11, /device:TPU:1, one launch (start us, length us, event | category | flops | bytes accessed | tf_op | source)
XLA Modules:
  0.0 102.7 jit_solution(3047796433958666469)
XLA Ops:
  0.0 0.7 iota_compare_fusion
  0.7 100.5 %shard_map.46 = bf16[4,64,128]{2,1,0:T(8,128)(2,1)} custom-call(bf16[4,64,128]{2,1,0:T(8,128)(2,1)} %amp_in.1, bf16[4,1280,128]{2,1,0:T(8,128)(2,1)} %vec.1, s32[4]{0:T(128)} %counts.1, s32[32,256]{1,0:T(8,128)} %bitcast.1), custom_call_target="tpu_custom_call" | custom-call | flops 12000000000 | bytes 4000000 | tf_op jit(solution)/shard_map/pallas_call | solution.py:535
  101.3 1.5 %broadcast_select_fusion = bf16[4,64,128]{2,1,0:T(8,128)(2,1)} fusion(bf16[4,64,128]{2,1,0:T(8,128)(2,1)} %shard_map.46, pred[4,128]{1,0:T(4,128)(4,1)S(1)} %iota_compare_fusion), kind=kLoop, calls=%fused_computation | loop fusion | flops 32768 | bytes 131584 | tf_op jit(solution)/shard_map/jit(_where)/select_n | solution.py:580
